TPU v7x, 128 devices: a whole 4x4x4 slice. The times are simulated.
128 devices in a mesh: section: 16 (over z_lo, x, core), ha: 2 (over z_hi), wa: 4 (over y).
Axes of the slice: x: 4, y: 4, z: 4 (z_hi: 2, z_lo: 2; z = z_hi * 2 + z_lo), core: 2. Of those that a mesh axis runs over, the one named last changes fastest.
Arguments:
- queries: bfloat16 [16, 4, 4, 8, 16, 2560], P('section', None, 'ha', 'wa'), may hold values from -28 to 28
- keys_values: bfloat16 [2, 16, 4, 4, 8, 16, 2560], P(None, 'section', None, 'ha', 'wa'), may hold values from -28 to 28
- grad_out: bfloat16 [16, 4, 4, 8, 16, 2560], P('section', None, 'ha', 'wa'), may hold values from -6 to 6
- time_start: int32 [4, 4, 8], P(None, 'ha', 'wa'), may hold values from 0 to 1, as said below
Outputs:
- grad_qkv: bfloat16 [3, 16, 4, 4, 8, 16, 2560], P(None, 'section', None, 'ha', 'wa')
Inputs may be any that keep to these rules, and one draw needn't show every extreme that they name: Each tile's window begins at most two tiles before the tile and never after it: max(0, t - 2) <= time_start[t, h, w] <= min(t, 1) for time index t.
All inputs are finite; a program needn't handle non-finite values.
Results may differ from a plain program's by a relative error of at most 0.012.
Values may be sent and summed in bfloat16 or wider, within the bound.
No kernel may reach another device: no remote copies, remote signals or barrier semaphores. Data moves between devices by JAX's collectives and lax.ppermute only.
A program may use at most 192 MiB of HBM per device.

v0:
```python
import functools

import jax
import jax.numpy as jnp
from jax import lax
from jax.experimental import pallas as pl
from jax.experimental.pallas import tpu as pltpu
from jax.sharding import PartitionSpec as P

HEAD_DIM = 128
SCALE = HEAD_DIM**-0.5
LOG2E = 1.4426950408889634
CHUNKS = (12, 8)
NEG = -1e30
GROUP = 2
BF = jnp.bfloat16
F32 = jnp.float32


def shift(block, axis, step):
    count = lax.axis_size(axis)
    return lax.ppermute(block, axis, [(i, (i + step) % count) for i in range(count)])


def shift_across(block):
    sections = lax.axis_size("section")
    route = []
    for i in range(sections):
        for h in range(2):
            route.append((i * 2 + h, (i - 1) % sections * 2 + 1 - h))
    return lax.ppermute(block, ("section", "ha"), route)


def nt(a, b):
    return lax.dot_general(a, b, (((1,), (1,)), ((), ())), preferred_element_type=F32)


def nn(a, b):
    return lax.dot_general(a, b, (((1,), (0,)), ((), ())), preferred_element_type=F32)


def tn(a, b):
    return lax.dot_general(a, b, (((0,), (0,)), ((), ())), preferred_element_type=F32)


def attend(
    base, place_ref, starts_ref, q_ref, g_ref, kv_ref, z_ref, xl_ref, xlc_ref, xr_ref, xrc_ref,
    dq_ref, own_ref, dz_ref, dxl_ref, dxlc_ref, dxr_ref, dxrc_ref,
):
    times = q_ref.shape[0]
    tok = q_ref.shape[3]
    heads = dq_ref.shape[4] // HEAD_DIM
    rows = times * 2 * tok
    n_kv, n_own, n_row = 2 * rows, 3 * rows, rows
    first = place_ref[0] == 0
    last = place_ref[0] == place_ref[1] - 1

    lane = lax.broadcasted_iota(jnp.int32, (1, rows), 1) // tok
    biases = []
    for j in range(2):
        start = jnp.zeros((1, rows), jnp.int32)
        for t in range(times):
            for h in range(2):
                start = jnp.where(lane == 2 * t + h, starts_ref[t, h, j], start)
        biases.append(
            [
                jnp.where((start <= t) & (t < start + 3), 0.0, NEG).astype(F32)
                for t in range(times)
            ]
        )

    def masked(scores, j):
        span = scores.shape[0] // times
        return [
            scores[t * span : (t + 1) * span] * (SCALE * LOG2E) + biases[j][t]
            for t in range(times)
        ]

    def load(index):
        cols = pl.ds(pl.multiple_of(index * HEAD_DIM, HEAD_DIM), HEAD_DIM)
        wide = pl.ds(pl.multiple_of((index + base) * HEAD_DIM, HEAD_DIM), HEAD_DIM)

        def flat(ref, *lead):
            lanes = wide if ref.shape[-1] == q_ref.shape[-1] else cols
            return ref[(*lead, lanes)].reshape(-1, HEAD_DIM)

        every = slice(None)
        q = jnp.concatenate([flat(q_ref, every, every, j, every) for j in range(2)], axis=0)
        g = jnp.concatenate([flat(g_ref, every, every, j, every) for j in range(2)], axis=0)
        own, side = [], []
        for s in range(2):
            own.append(
                jnp.concatenate(
                    [
                        flat(kv_ref, s, every, every, every, every),
                        flat(z_ref, s, every, every, every),
                    ],
                    axis=0,
                )
            )
            left = jnp.concatenate(
                [flat(xl_ref, s, every, every, every), flat(xlc_ref, s, every, every)], axis=0
            )
            right = jnp.concatenate(
                [flat(xr_ref, s, every, every, every), flat(xrc_ref, s, every, every)], axis=0
            )
            side.append((jnp.where(first, right, left), jnp.where(last, left, right)))
        return q, g, own, side

    def half(value, j):
        return value[j * rows : (j + 1) * rows]

    def products(loaded):
        q, g, own, side = loaded
        return (
            nt(own[0], q),
            nt(own[1], g),
            [nt(side[0][j], half(q, j)) for j in range(2)],
            [nt(side[1][j], half(g, j)) for j in range(2)],
        )

    def soften(made):
        s_own, p_own, s_x, p_x = made
        low_out, ds_out = [], []
        for j in range(2):
            lanes = slice(j * rows, (j + 1) * rows)
            parts = [s_own[:n_kv, lanes], s_own[n_kv:, lanes], s_x[j][:n_row], s_x[j][n_row:]]
            scores = jnp.concatenate(sum([masked(part, j) for part in parts], []), axis=0)
            grads = jnp.concatenate([p_own[:, lanes], p_x[j]], axis=0)
            top = jnp.max(scores, axis=0, keepdims=True)
            weights = jnp.exp2(scores - top)
            inverse = 1.0 / jnp.sum(weights, axis=0, keepdims=True)
            delta = jnp.sum(weights * grads, axis=0, keepdims=True) * inverse
            probs = weights * inverse
            low_out.append(probs.astype(BF))
            ds_out.append((probs * (grads - delta)).astype(BF))
        return low_out, ds_out

    def gradients(loaded, soft):
        q, g, own, side = loaded
        low, ds = soft
        d_own = (
            nn(jnp.concatenate([ds[0][:n_own], ds[1][:n_own]], axis=1), q) * SCALE,
            nn(jnp.concatenate([low[0][:n_own], low[1][:n_own]], axis=1), g),
        )
        dk_x = [nn(ds[j][n_own:], half(q, j)) * SCALE for j in range(2)]
        dv_x = [nn(low[j][n_own:], half(g, j)) for j in range(2)]
        dq = []
        for j in range(2):
            keys = jnp.concatenate([own[0], side[0][j]], axis=0)
            dq.append((tn(ds[j], keys) * SCALE).astype(BF))
        return d_own, (dk_x, dv_x), dq

    def store(cols, made):
        d_own, d_x, dq = made
        for j in range(2):
            dq_ref[:, :, j, :, cols] = dq[j].reshape(times, 2, tok, HEAD_DIM)
        for s in range(2):
            own_ref[s, :, :, :, :, cols] = (
                d_own[s][:n_kv].reshape(times, 2, 2, tok, HEAD_DIM).astype(own_ref.dtype)
            )
            dz_ref[s, :, :, :, cols] = d_own[s][n_kv:].reshape(times, 2, tok, HEAD_DIM)
            d0, d1 = d_x[s]
            left = (jnp.where(first, 0.0, d0) + jnp.where(last, d1, 0.0)).astype(BF)
            right = (jnp.where(last, 0.0, d1) + jnp.where(first, d0, 0.0)).astype(BF)
            for value, ref, corner in ((left, dxl_ref, dxlc_ref), (right, dxr_ref, dxrc_ref)):
                ref[s, :, :, :, cols] = value[:n_row].reshape(times, 2, tok, HEAD_DIM)
                corner[s, :, :, cols] = value[n_row:].reshape(times, tok, HEAD_DIM)

    def step(index, carry):
        each = [index * GROUP + i for i in range(GROUP)]
        loaded = [load(i) for i in each]
        made = [products(x) for x in loaded]
        soft = [soften(x) for x in made]
        done = [gradients(x, y) for x, y in zip(loaded, soft)]
        for i, d in zip(each, done):
            store(pl.ds(pl.multiple_of(i * HEAD_DIM, HEAD_DIM), HEAD_DIM), d)
        return carry

    lax.fori_loop(0, heads // GROUP, step, 0)


def corner_sum(dz_ref, c0_ref, c1_ref, out_ref):
    for j, ref in enumerate((c0_ref, c1_ref)):
        out_ref[:, :, j] = (dz_ref[:, :, j] + ref[...].astype(F32)).astype(BF)


def own_sum(own_ref, r0_ref, r1_ref, out_ref):
    for s in range(2):
        for j, ref in enumerate((r0_ref, r1_ref)):
            out_ref[s, :, :, j] = (own_ref[s, :, :, j] + ref[s].astype(F32)).astype(BF)


VMEM = pl.BlockSpec(memory_space=pltpu.VMEM)
SMEM = pl.BlockSpec(memory_space=pltpu.SMEM)


def call(body, specs, shapes, name, flops=0, moved=0, exps=0):
    single = not isinstance(shapes, (list, tuple))
    return pl.pallas_call(
        body,
        in_specs=specs,
        out_specs=VMEM if single else [VMEM] * len(shapes),
        out_shape=shapes,
        name=name,
        compiler_params=pltpu.CompilerParams(vmem_limit_bytes=58 * 2**20),
        cost_estimate=pl.CostEstimate(flops=flops, bytes_accessed=moved, transcendentals=exps),
    )


def local(queries, keys_values, grad_out, starts):
    queries, keys_values, grad_out = queries[0], keys_values[:, 0], grad_out[0]
    times, _, _, tok, channels = queries.shape
    row = lax.axis_index("ha")
    col = lax.axis_index("wa")
    col_place = jnp.stack([col, lax.axis_size("wa")]).astype(jnp.int32)
    sd = jax.ShapeDtypeStruct
    edge_row = lax.dynamic_index_in_dim(keys_values, 1 - row, axis=2, keepdims=False)

    halos = []
    base = 0
    own_done = z_done = corners_first = None
    for heads in CHUNKS:
        lanes = slice(base * HEAD_DIM, (base + heads) * HEAD_DIM)
        to_left = keys_values[:, :, :, 0, :, lanes]
        to_right = keys_values[:, :, :, 1, :, lanes]
        z_send = edge_row[..., lanes]
        if own_done is not None:
            gate = corners_first
            to_left, to_right, gate = lax.optimization_barrier((to_left, to_right, gate))
            z_send, z_done = lax.optimization_barrier((z_send, z_done))
        xr = shift(to_left, "wa", -1)
        xl = shift(to_right, "wa", 1)
        own_done = True
        z_row = z_done = shift(z_send, "ha", 1)
        if corners_first is None:
            xrc = shift(z_row[:, :, 0], "wa", -1)
            xlc = shift(z_row[:, :, 1], "wa", 1)
            corners_first = (xrc, xlc)
        halos.append((base, heads, z_row, xl, xr))
        base += heads

    made = []
    for index, (base, heads, z_row, xl, xr) in enumerate(halos):
        if index == 0:
            xrc, xlc = corners_first
        else:
            z_row, dq = lax.optimization_barrier((z_row, made[-1][0]))
            made[-1] = (dq, *made[-1][1:])
            xrc = shift(z_row[:, :, 0], "wa", -1)
            xlc = shift(z_row[:, :, 1], "wa", 1)
        width = heads * HEAD_DIM
        body = (times, 2, tok, width)
        outs = call(
            functools.partial(attend, base),
            [SMEM, SMEM] + [VMEM] * 8,
            [
                sd((times, 2, 2, tok, width), BF),
                sd((2, times, 2, 2, tok, width), F32),
                sd((2, *body), F32),
                sd((2, *body), BF),
                sd((2, times, tok, width), BF),
                sd((2, *body), BF),
                sd((2, times, tok, width), BF),
            ],
            "attend",
            flops=2 * 10**8 * heads,
            moved=2**20 * heads,
            exps=150000 * heads,
        )(col_place, starts, queries, grad_out, keys_values, z_row, xl, xlc, xr, xrc)
        made.append(outs)
    query_parts, pair_parts, across_parts = [], [], []
    z_back = total = None
    for index, (dq, own, dz, dxl, dxlc, dxr, dxrc) in enumerate(made):
        width = own.shape[-1]
        body = (times, 2, tok, width)
        query_part = shift(dq, "section", -1)
        if z_back is not None:
            dxlc, dxrc, z_back = lax.optimization_barrier((dxlc, dxrc, z_back))
            dxl, dxr, total = lax.optimization_barrier((dxl, dxr, total))
        r1c = shift(dxlc, "wa", -1)
        r0c = shift(dxrc, "wa", 1)
        r1 = shift(dxl, "wa", -1)
        r0 = shift(dxr, "wa", 1)
        z_back = call(corner_sum, [VMEM] * 3, sd((2, *body), BF), "corner_sum", moved=4 * 2**20)(
            dz, r0c, r1c
        )
        across = shift_across(z_back)
        held = (r0, r1, query_part, *across_parts)
        r0, r1, query_part, *across_parts = lax.optimization_barrier(held)
        total = call(
            own_sum, [VMEM] * 3, sd((2, times, 2, 2, tok, width), BF), "own_sum", moved=5 * 2**20
        )(own, r0, r1)
        query_parts.append(query_part)
        across_parts.append(across)
        pair_parts.append(shift(total, "section", -1))
    across = jnp.concatenate(across_parts, axis=-1)[:, :, None].astype(F32)
    pair = jnp.concatenate(pair_parts, axis=-1).astype(F32)
    at_edge = lax.broadcasted_iota(jnp.int32, (1, 1, 2, 1, 1, 1), 2) == 1 - row
    pair = (pair + jnp.where(at_edge, across, 0.0)).astype(BF)
    rows = [jnp.concatenate(query_parts, axis=-1)[None], pair]
    return jnp.concatenate(rows, axis=0)[:, None]


def solution(mesh):
    return jax.shard_map(
        local,
        mesh=mesh,
        in_specs=(
            P("section", None, "ha", "wa", None, None),
            P(None, "section", None, "ha", "wa", None, None),
            P("section", None, "ha", "wa", None, None),
            P(None, "ha", "wa"),
        ),
        out_specs=P(None, "section", None, "ha", "wa", None, None),
        check_vma=False,
    )
```

profile of v0, /device:TPU:6, one launch (start us, length us, event | category | flops | bytes accessed | tf_op | source)
XLA Modules:
  0.0 154.5 jit_solution(5703555108468942883)
XLA Ops:
  0.0 1.6 %copy_bitcast_fusion.1 = bf16[2,4,2,16,2560]{4,3,1,0,2:T(8,128)(2,1)S(1)} fusion(bf16[2,1,4,2,2,16,2560]{6,5,4,3,2,1,0:T(8,128)(2,1)} %param.5, s32[]{:T(128)S(6)} %select_n.8), kind=kLoop, calls=%fused_computation.5 | loop fusion | bytes 2621444 | tf_op jit(solution)/shard_map/jit(dynamic_index_in_dim)/squeeze | solution.py:218
  1.6 4.0 %collective-permute-start = (bf16[2,4,2,16,1536]{4,3,1,0,2:T(8,128)(2,1)S(1)}, bf16[2,4,2,16,1536]{4,3,1,0,2:T(8,128)(2,1)S(1)}, u32[]{:S(2)}, u32[]{:S(2)}) collective-permute-start(bf16[2,4,2,16,1536]{4,3,1,0,2:T(8,128)(2,1)S(1)} %slice.40), channel_id=1, source_target_pairs={{0,4},{4,0},{1,5},{5,1},{2,6},{6,2},{3,7},{7,3},{8,12},{12,8},{9,1... | collective-permute-start | bytes 2359304 | tf_op jit(solution)/shard_map/ppermute | solution.py:22
  5.6 0.2 copy.17
  5.8 0.1 slice_bitcast_fusion
  5.9 3.1 %collective-permute-start.3 = (bf16[2,4,2,16,1536]{4,3,2,1,0:T(8,128)(2,1)S(1)}, bf16[2,4,2,16,1536]{4,3,2,1,0:T(8,128)(2,1)}, u32[]{:S(2)}, u32[]{:S(2)}) collective-permute-start(bf16[2,4,2,16,1536]{4,3,2,1,0:T(8,128)(2,1)S(1)} %get-tuple-element.67), channel_id=1, source_target_pairs={{0,3},{1,0},{2,1},{3,2},{4,7},{5,4},{6,5},{7,6},{8,11},{9,8},{10,9... | collective-permute-start | bytes 2359304 | tf_op jit(solution)/shard_map/ppermute | solution.py:22
  9.0 14.1 %collective-permute-done = bf16[2,4,2,16,1536]{4,3,1,0,2:T(8,128)(2,1)S(1)} collective-permute-done((bf16[2,4,2,16,1536]{4,3,1,0,2:T(8,128)(2,1)S(1)}, bf16[2,4,2,16,1536]{4,3,1,0,2:T(8,128)(2,1)S(1)}, u32[]{:S(2)}, u32[]{:S(2)}) %collective-permute-start) | collective-permute-done | bytes 786464 | tf_op jit(solution)/shard_map/ppermute | solution.py:22
  23.1 0.9 slice_bitcast_fusion.4
  24.0 3.0 %collective-permute-start.4 = (bf16[2,4,16,1536]{3,2,1,0:T(8,128)(2,1)}, bf16[2,4,16,1536]{3,2,1,0:T(8,128)(2,1)}, u32[]{:S(2)}, u32[]{:S(2)}) collective-permute-start(bf16[2,4,16,1536]{3,2,1,0:T(8,128)(2,1)} %get-tuple-element.69), channel_id=1, source_target_pairs={{0,3},{1,0},{2,1},{3,2},{4,7},{5,4},{6,5},{7,6},{8,11},{9,8},{10,9... | collective-permute-start | bytes 1179656 | tf_op jit(solution)/shard_map/ppermute | solution.py:22
  27.1 3.3 %collective-permute-start.7 = (bf16[2,4,2,16,1024]{4,3,1,0,2:T(8,128)(2,1)S(1)}, bf16[2,4,2,16,1024]{4,3,1,0,2:T(8,128)(2,1)S(1)}, u32[]{:S(2)}, u32[]{:S(2)}) collective-permute-start(bf16[2,4,2,16,1024]{4,3,1,0,2:T(8,128)(2,1)S(1)} %slice.45), channel_id=1, source_target_pairs={{0,4},{4,0},{1,5},{5,1},{2,6},{6,2},{3,7},{7,3},{8,12},{12,8},{9,1... | collective-permute-start | bytes 1572872 | tf_op jit(solution)/shard_map/ppermute | solution.py:22
  30.5 0.7 copy.7.starts_ref
  31.1 0.6 pad_add_fusion.place_ref
  31.7 0.9 copy.9.z_ref
  32.7 2.5 %collective-permute-done.4.xrc_ref = bf16[2,4,16,1536]{3,2,1,0:T(8,128)(2,1)} collective-permute-done((bf16[2,4,16,1536]{3,2,1,0:T(8,128)(2,1)}, bf16[2,4,16,1536]{3,2,1,0:T(8,128)(2,1)}, u32[]{:S(2)}, u32[]{:S(2)}) %collective-permute-start.4) | collective-permute-done | bytes 393248 | tf_op jit(solution)/shard_map/ppermute | solution.py:22
  35.2 3.4 %collective-permute-done.2.xlc_ref = bf16[2,4,16,1536]{3,2,1,0:T(8,128)(2,1)} collective-permute-done((bf16[2,4,16,1536]{3,2,1,0:T(8,128)(2,1)}, bf16[2,4,16,1536]{3,2,1,0:T(8,128)(2,1)}, u32[]{:S(2)}, u32[]{:S(2)}) %collective-permute-start.2) | collective-permute-done | bytes 393248 | tf_op jit(solution)/shard_map/ppermute | solution.py:22
  38.6 14.4 %attend.2 = (bf16[4,2,2,16,1536]{4,3,2,1,0:T(8,128)(2,1)}, f32[2,4,2,2,16,1536]{5,4,3,2,1,0:T(8,128)}, f32[2,4,2,16,1536]{4,3,2,1,0:T(8,128)}, bf16[2,4,2,16,153...) custom-call(s32[2]{0:T(128)} %pad_add_fusion.place_ref, ...), custom_call_target="tpu_custom_call" | custom-call | flops 2400000000 | bytes 12582912 | tf_op jit(solution)/shard_map/attend/pallas_call | solution.py:254
  53.1 3.2 %collective-permute-start.17 = (bf16[2,4,16,1536]{3,2,1,0:T(8,128)(2,1)}, bf16[2,4,16,1536]{3,2,1,0:T(8,128)(2,1)S(1)}, u32[]{:S(2)}, u32[]{:S(2)}) collective-permute-start(bf16[2,4,16,1536]{3,2,1,0:T(8,128)(2,1)} %get-tuple-element.54), channel_id=1, source_target_pairs={{0,3},{1,0},{2,1},{3,2},{4,7},{5,4},{6,5},{7,6},{8,11},{9,8},{10,9... | collective-permute-start | bytes 1179656 | tf_op jit(solution)/shard_map/ppermute | solution.py:22
  56.3 0.1 collective-permute-start.12
  56.4 2.0 %collective-permute-start.10 = (bf16[2,4,16,1024]{3,2,1,0:T(8,128)(2,1)S(1)}, bf16[2,4,16,1024]{3,2,1,0:T(8,128)(2,1)}, u32[]{:S(2)}, u32[]{:S(2)}) collective-permute-start(bf16[2,4,16,1024]{3,2,1,0:T(8,128)(2,1)S(1)} %get-tuple-element.72), channel_id=1, source_target_pairs={{0,1},{1,2},{2,3},{3,0},{4,5},{5,6},{6,7},{7,4},{8,9},{9,10},{10,1... | collective-permute-start | bytes 786440 | tf_op jit(solution)/shard_map/ppermute | solution.py:22
  58.4 1.3 slice_bitcast_fusion.2
  59.8 6.7 %collective-permute-done.16.c0_ref = bf16[2,4,16,1536]{3,2,1,0:T(8,128)(2,1)S(1)} collective-permute-done((bf16[2,4,16,1536]{3,2,1,0:T(8,128)(2,1)}, bf16[2,4,16,1536]{3,2,1,0:T(8,128)(2,1)S(1)}, u32[]{:S(2)}, u32[]{:S(2)}) %collective-permute-start.16) | collective-permute-done | bytes 393248 | tf_op jit(solution)/shard_map/ppermute | solution.py:22
  66.5 2.0 %collective-permute-start.5 = (bf16[2,4,2,16,1536]{4,3,2,1,0:T(8,128)(2,1)}, bf16[2,4,2,16,1536]{4,3,2,1,0:T(8,128)(2,1)S(1)}, u32[]{:S(2)}, u32[]{:S(2)}) collective-permute-start(bf16[2,4,2,16,1536]{4,3,2,1,0:T(8,128)(2,1)} %get-tuple-element.35), channel_id=1, source_target_pairs={{0,1},{1,2},{2,3},{3,0},{4,5},{5,6},{6,7},{7,4},{8,9},{9,10},{10,1... | collective-permute-start | bytes 2359304 | tf_op jit(solution)/shard_map/ppermute | solution.py:22
  68.6 3.1 %collective-permute-done.12.xrc_ref = bf16[2,4,16,1024]{3,2,1,0:T(8,128)(2,1)S(1)} collective-permute-done((bf16[2,4,16,1024]{3,2,1,0:T(8,128)(2,1)S(1)}, bf16[2,4,16,1024]{3,2,1,0:T(8,128)(2,1)S(1)}, u32[]{:S(2)}, u32[]{:S(2)}) %collective-permute-start.12) | collective-permute-done | bytes 262176 | tf_op jit(solution)/shard_map/ppermute | solution.py:22
  71.7 3.7 %collective-permute-start.6 = (bf16[2,4,2,16,1536]{4,3,2,1,0:T(8,128)(2,1)}, bf16[2,4,2,16,1536]{4,3,2,1,0:T(8,128)(2,1)S(1)}, u32[]{:S(2)}, u32[]{:S(2)}) collective-permute-start(bf16[2,4,2,16,1536]{4,3,2,1,0:T(8,128)(2,1)} %get-tuple-element.36), channel_id=1, source_target_pairs={{0,3},{1,0},{2,1},{3,2},{4,7},{5,4},{6,5},{7,6},{8,11},{9,8},{10,9... | collective-permute-start | bytes 2359304 | tf_op jit(solution)/shard_map/ppermute | solution.py:22
  75.4 2.6 %corner_sum.2 = bf16[2,4,2,16,1536]{4,3,2,1,0:T(8,128)(2,1)} custom-call(f32[2,4,2,16,1536]{4,3,2,1,0:T(8,128)} %get-tuple-element.52.dz_ref, bf16[2,4,16,1536]{3,2,1,0:T(8,128)(2,1)} %copy-done.8, bf16[2,4,16,1536]{3,2,1,0:T(8,128)(2,1)} %copy-done.9), custom_call_target="tpu_custom_call" | custom-call | bytes 4194304 | tf_op jit(solution)/shard_map/corner_sum/pallas_call | solution.py:285
  78.0 5.4 %collective-permute-done.9.xl_ref = bf16[2,4,2,16,1024]{4,3,2,1,0:T(8,128)(2,1)S(1)} collective-permute-done((bf16[2,4,2,16,1024]{4,3,2,1,0:T(8,128)(2,1)S(1)}, bf16[2,4,2,16,1024]{4,3,2,1,0:T(8,128)(2,1)S(1)}, u32[]{:S(2)}, u32[]{:S(2)}) %collective-permute-start.9) | collective-permute-done | bytes 524320 | tf_op jit(solution)/shard_map/ppermute | solution.py:22
  83.4 0.9 copy.12.z_ref
  84.4 0.8 copy-done.5
  85.1 10.8 %attend.3 = (bf16[4,2,2,16,1024]{4,3,2,1,0:T(8,128)(2,1)}, f32[2,4,2,2,16,1024]{5,4,3,2,1,0:T(8,128)}, f32[2,4,2,16,1024]{4,3,2,1,0:T(8,128)}, bf16[2,4,2,16,102...) custom-call(s32[2]{0:T(128)} %pad_add_fusion.place_ref, ...), custom_call_target="tpu_custom_call" | custom-call | flops 1600000000 | bytes 8388608 | tf_op jit(solution)/shard_map/attend/pallas_call | solution.py:254
  95.9 3.5 %collective-permute-start.15 = (bf16[4,2,2,16,1024]{4,3,2,1,0:T(8,128)(2,1)}, bf16[4,2,2,16,1024]{4,3,2,1,0:T(8,128)(2,1)S(1)}, u32[]{:S(2)}, u32[]{:S(2)}) collective-permute-start(bf16[4,2,2,16,1024]{4,3,2,1,0:T(8,128)(2,1)} %get-tuple-element.51), channel_id=1, source_target_pairs={{0,120},{8,0},{16,8},{24,16},{32,24},{40,32},{48,40},{56,48},{64,5... | collective-permute-start | bytes 1572872 | tf_op jit(solution)/shard_map/ppermute | solution.py:22
  99.5 0.9 copy-done.2
  100.3 0.2 copy-done.3
  100.6 3.8 %own_sum.2 = bf16[2,4,2,2,16,1536]{5,4,3,2,1,0:T(8,128)(2,1)} custom-call(f32[2,4,2,2,16,1536]{5,4,3,2,1,0:T(8,128)} %get-tuple-element.46.own_ref, bf16[2,4,2,16,1536]{4,3,2,1,0:T(8,128)(2,1)} %copy-done.2, bf16[2,4,2,16,1536]{4,3,2,1,0:T(8,128)(2,1)} %copy-done.3), custom_call_target="tpu_custom_call" | custom-call | bytes 5242880 | tf_op jit(solution)/shard_map/own_sum/pallas_call | solution.py:291
  104.4 3.2 %collective-permute-start.14 = (bf16[2,4,2,16,1024]{4,3,2,1,0:T(8,128)(2,1)S(1)}, bf16[2,4,2,16,1024]{4,3,2,1,0:T(8,128)(2,1)S(1)}, u32[]{:S(2)}, u32[]{:S(2)}) collective-permute-start(bf16[2,4,2,16,1024]{4,3,2,1,0:T(8,128)(2,1)S(1)} %copy-done.14), channel_id=1, source_target_pairs={{0,3},{1,0},{2,1},{3,2},{4,7},{5,4},{6,5},{7,6},{8,11},{9,8},{10,9... | collective-permute-start | bytes 1572872 | tf_op jit(solution)/shard_map/ppermute | solution.py:22
  107.7 3.2 %collective-permute-done.18 = bf16[2,4,2,16,1536]{4,3,2,1,0:T(8,128)(2,1)S(1)} collective-permute-done((bf16[2,4,2,16,1536]{4,3,2,1,0:T(8,128)(2,1)}, bf16[2,4,2,16,1536]{4,3,2,1,0:T(8,128)(2,1)S(1)}, u32[]{:S(2)}, u32[]{:S(2)}) %collective-permute-start.18) | collective-permute-done | bytes 786464 | tf_op jit(solution)/shard_map/ppermute | solution.py:31
  111.0 9.7 %collective-permute-done.13.r0_ref = bf16[2,4,2,16,1024]{4,3,2,1,0:T(8,128)(2,1)S(1)} collective-permute-done((bf16[2,4,2,16,1024]{4,3,2,1,0:T(8,128)(2,1)}, bf16[2,4,2,16,1024]{4,3,2,1,0:T(8,128)(2,1)S(1)}, u32[]{:S(2)}, u32[]{:S(2)}) %collective-permute-start.13) | collective-permute-done | bytes 524320 | tf_op jit(solution)/shard_map/ppermute | solution.py:22
  120.7 0.8 copy-done.6
  121.5 0.2 copy-done.7
  121.7 3.0 %own_sum.3 = bf16[2,4,2,2,16,1024]{5,4,3,2,1,0:T(8,128)(2,1)} custom-call(f32[2,4,2,2,16,1024]{5,4,3,2,1,0:T(8,128)} %get-tuple-element.56.own_ref, bf16[2,4,2,16,1024]{4,3,2,1,0:T(8,128)(2,1)} %copy-done.6, bf16[2,4,2,16,1024]{4,3,2,1,0:T(8,128)(2,1)} %copy-done.7), custom_call_target="tpu_custom_call" | custom-call | bytes 5242880 | tf_op jit(solution)/shard_map/own_sum/pallas_call | solution.py:291
  124.6 0.2 collective-permute-done.21.c0_ref
  124.9 0.7 copy-done.11
  125.6 0.1 copy-done.12
  125.7 2.2 %corner_sum.3 = bf16[2,4,2,16,1024]{4,3,2,1,0:T(8,128)(2,1)} custom-call(f32[2,4,2,16,1024]{4,3,2,1,0:T(8,128)} %get-tuple-element.60.dz_ref, bf16[2,4,16,1024]{3,2,1,0:T(8,128)(2,1)} %copy-done.11, bf16[2,4,16,1024]{3,2,1,0:T(8,128)(2,1)} %copy-done.12), custom_call_target="tpu_custom_call" | custom-call | bytes 4194304 | tf_op jit(solution)/shard_map/corner_sum/pallas_call | solution.py:285
  127.9 0.8 collective-permute-start.23
  128.7 0.1 maximum_bitcast_fusion.1
  128.8 22.2 %collective-permute-done.23 = bf16[2,4,2,16,1024]{4,3,2,1,0:T(8,128)(2,1)S(1)} collective-permute-done((bf16[2,4,2,16,1024]{4,3,2,1,0:T(8,128)(2,1)}, bf16[2,4,2,16,1024]{4,3,2,1,0:T(8,128)(2,1)S(1)}, u32[]{:S(2)}, u32[]{:S(2)}) %collective-permute-start.23) | collective-permute-done | bytes 524320 | tf_op jit(solution)/shard_map/ppermute | solution.py:31
  151.0 0.3 maximum_convert_fusion
  151.4 0.9 add_convert_fusion
  152.2 2.3 %maximum_bitcast_fusion = bf16[3,1,4,2,2,16,2560]{6,5,4,3,2,1,0:T(8,128)(2,1)} fusion(bf16[2,4,2,2,16,2560]{5,4,3,2,1,0:T(8,128)(2,1)S(1)} %add_convert_fusion, bf16[1,4,2,2,16,2560]{5,4,3,2,1,0:T(8,128)(2,1)S(1)} %maximum_bitcast_fusion.1), kind=kLoop, calls=%fused_computation.1 | loop fusion | flops 1966080 | bytes 7864320 | tf_op jit(solution)/shard_map/broadcast_in_dim | solution.py:302
  (55 shorter events, 0.5 us)
Async XLA Ops:
  0.0 5.6 %copy-start = (bf16[2,1,4,2,2,16,2560]{6,5,4,3,2,1,0:T(8,128)(2,1)S(1)}, bf16[2,1,4,2,2,16,2560]{6,5,4,3,2,1,0:T(8,128)(2,1)}, u32[]{:S(2)}) copy-start(bf16[2,1,4,2,2,16,2560]{6,5,4,3,2,1,0:T(8,128)(2,1)} %param.5) | copy-start | bytes 7864324
  1.6 21.5 %collective-permute-start = (bf16[2,4,2,16,1536]{4,3,1,0,2:T(8,128)(2,1)S(1)}, bf16[2,4,2,16,1536]{4,3,1,0,2:T(8,128)(2,1)S(1)}, u32[]{:S(2)}, u32[]{:S(2)}) collective-permute-start(bf16[2,4,2,16,1536]{4,3,1,0,2:T(8,128)(2,1)S(1)} %slice.40), channel_id=1, source_target_pairs={{0,4},{4,0},{1,5},{5,1},{2,6},{6,2},{3,7},{7,3},{8,12},{12,8},{9,1... | collective-permute-start | bytes 2359304 | tf_op jit(solution)/shard_map/ppermute | solution.py:22
  5.8 21.4 %copy-start.1 = (bf16[2,1,4,2,2,16,2560]{6,5,3,2,0,4,1:T(8,128)(2,1)}, bf16[2,1,4,2,2,16,2560]{6,5,3,2,0,4,1:T(8,128)(2,1)S(1)}, u32[]{:S(2)}) copy-start(bf16[2,1,4,2,2,16,2560]{6,5,3,2,0,4,1:T(8,128)(2,1)S(1)} %copy.17) | copy-start | bytes 7864324
  5.8 24.7 %copy-start.13 = (s32[4,2,2]{0,2,1:T(2,128)S(1)}, s32[4,2,2]{0,2,1:T(2,128)}, u32[]{:S(2)}) copy-start(s32[4,2,2]{0,2,1:T(2,128)} %param.7) | copy-start | bytes 196
  5.9 26.8 %collective-permute-start.3 = (bf16[2,4,2,16,1536]{4,3,2,1,0:T(8,128)(2,1)S(1)}, bf16[2,4,2,16,1536]{4,3,2,1,0:T(8,128)(2,1)}, u32[]{:S(2)}, u32[]{:S(2)}) collective-permute-start(bf16[2,4,2,16,1536]{4,3,2,1,0:T(8,128)(2,1)S(1)} %get-tuple-element.67), channel_id=1, source_target_pairs={{0,3},{1,0},{2,1},{3,2},{4,7},{5,4},{6,5},{7,6},{8,11},{9,8},{10,9... | collective-permute-start | bytes 2359304 | tf_op jit(solution)/shard_map/ppermute | solution.py:22
  9.0 23.7 %collective-permute-start.1 = (bf16[2,4,2,16,1536]{4,3,2,1,0:T(8,128)(2,1)S(1)}, bf16[2,4,2,16,1536]{4,3,2,1,0:T(8,128)(2,1)}, u32[]{:S(2)}, u32[]{:S(2)}) collective-permute-start(bf16[2,4,2,16,1536]{4,3,2,1,0:T(8,128)(2,1)S(1)} %get-tuple-element.68), channel_id=1, source_target_pairs={{0,1},{1,2},{2,3},{3,0},{4,5},{5,6},{6,7},{7,4},{8,9},{9,10},{10,1... | collective-permute-start | bytes 2359304 | tf_op jit(solution)/shard_map/ppermute | solution.py:22
  24.0 11.2 %collective-permute-start.4 = (bf16[2,4,16,1536]{3,2,1,0:T(8,128)(2,1)}, bf16[2,4,16,1536]{3,2,1,0:T(8,128)(2,1)}, u32[]{:S(2)}, u32[]{:S(2)}) collective-permute-start(bf16[2,4,16,1536]{3,2,1,0:T(8,128)(2,1)} %get-tuple-element.69), channel_id=1, source_target_pairs={{0,3},{1,0},{2,1},{3,2},{4,7},{5,4},{6,5},{7,6},{8,11},{9,8},{10,9... | collective-permute-start | bytes 1179656 | tf_op jit(solution)/shard_map/ppermute | solution.py:22
  27.1 11.5 %collective-permute-start.2 = (bf16[2,4,16,1536]{3,2,1,0:T(8,128)(2,1)}, bf16[2,4,16,1536]{3,2,1,0:T(8,128)(2,1)}, u32[]{:S(2)}, u32[]{:S(2)}) collective-permute-start(bf16[2,4,16,1536]{3,2,1,0:T(8,128)(2,1)} %get-tuple-element.70), channel_id=1, source_target_pairs={{0,1},{1,2},{2,3},{3,0},{4,5},{5,6},{6,7},{7,4},{8,9},{9,10},{10,1... | collective-permute-start | bytes 1179656 | tf_op jit(solution)/shard_map/ppermute | solution.py:22
  27.1 29.2 %collective-permute-start.7 = (bf16[2,4,2,16,1024]{4,3,1,0,2:T(8,128)(2,1)S(1)}, bf16[2,4,2,16,1024]{4,3,1,0,2:T(8,128)(2,1)S(1)}, u32[]{:S(2)}, u32[]{:S(2)}) collective-permute-start(bf16[2,4,2,16,1024]{4,3,1,0,2:T(8,128)(2,1)S(1)} %slice.45), channel_id=1, source_target_pairs={{0,4},{4,0},{1,5},{5,1},{2,6},{6,2},{3,7},{7,3},{8,12},{12,8},{9,1... | collective-permute-start | bytes 1572872 | tf_op jit(solution)/shard_map/ppermute | solution.py:22
  53.0 13.5 %collective-permute-start.16 = (bf16[2,4,16,1536]{3,2,1,0:T(8,128)(2,1)}, bf16[2,4,16,1536]{3,2,1,0:T(8,128)(2,1)S(1)}, u32[]{:S(2)}, u32[]{:S(2)}) collective-permute-start(bf16[2,4,16,1536]{3,2,1,0:T(8,128)(2,1)} %get-tuple-element.53), channel_id=1, source_target_pairs={{0,1},{1,2},{2,3},{3,0},{4,5},{5,6},{6,7},{7,4},{8,9},{9,10},{10,1... | collective-permute-start | bytes 1179656 | tf_op jit(solution)/shard_map/ppermute | solution.py:22
  53.1 13.5 %collective-permute-start.17 = (bf16[2,4,16,1536]{3,2,1,0:T(8,128)(2,1)}, bf16[2,4,16,1536]{3,2,1,0:T(8,128)(2,1)S(1)}, u32[]{:S(2)}, u32[]{:S(2)}) collective-permute-start(bf16[2,4,16,1536]{3,2,1,0:T(8,128)(2,1)} %get-tuple-element.54), channel_id=1, source_target_pairs={{0,3},{1,0},{2,1},{3,2},{4,7},{5,4},{6,5},{7,6},{8,11},{9,8},{10,9... | collective-permute-start | bytes 1179656 | tf_op jit(solution)/shard_map/ppermute | solution.py:22
  56.3 15.3 %collective-permute-start.12 = (bf16[2,4,16,1024]{3,2,1,0:T(8,128)(2,1)S(1)}, bf16[2,4,16,1024]{3,2,1,0:T(8,128)(2,1)S(1)}, u32[]{:S(2)}, u32[]{:S(2)}) collective-permute-start(bf16[2,4,16,1024]{3,2,1,0:T(8,128)(2,1)S(1)} %get-tuple-element.71), channel_id=1, source_target_pairs={{0,3},{1,0},{2,1},{3,2},{4,7},{5,4},{6,5},{7,6},{8,11},{9,8},{10,9... | collective-permute-start | bytes 786440 | tf_op jit(solution)/shard_map/ppermute | solution.py:22
  56.4 19.0 %collective-permute-start.10 = (bf16[2,4,16,1024]{3,2,1,0:T(8,128)(2,1)S(1)}, bf16[2,4,16,1024]{3,2,1,0:T(8,128)(2,1)}, u32[]{:S(2)}, u32[]{:S(2)}) collective-permute-start(bf16[2,4,16,1024]{3,2,1,0:T(8,128)(2,1)S(1)} %get-tuple-element.72), channel_id=1, source_target_pairs={{0,1},{1,2},{2,3},{3,0},{4,5},{5,6},{6,7},{7,4},{8,9},{9,10},{10,1... | collective-permute-start | bytes 786440 | tf_op jit(solution)/shard_map/ppermute | solution.py:22
  59.7 23.7 %collective-permute-start.9 = (bf16[2,4,2,16,1024]{4,3,2,1,0:T(8,128)(2,1)S(1)}, bf16[2,4,2,16,1024]{4,3,2,1,0:T(8,128)(2,1)S(1)}, u32[]{:S(2)}, u32[]{:S(2)}) collective-permute-start(bf16[2,4,2,16,1024]{4,3,2,1,0:T(8,128)(2,1)S(1)} %get-tuple-element.42), channel_id=1, source_target_pairs={{0,1},{1,2},{2,3},{3,0},{4,5},{5,6},{6,7},{7,4},{8,9},{9,10},{10,1... | collective-permute-start | bytes 1572872 | tf_op jit(solution)/shard_map/ppermute | solution.py:22
  66.5 8.9 %copy-start.8 = (bf16[2,4,16,1536]{3,2,1,0:T(8,128)(2,1)}, bf16[2,4,16,1536]{3,2,1,0:T(8,128)(2,1)S(1)}, u32[]{:S(2)}) copy-start(bf16[2,4,16,1536]{3,2,1,0:T(8,128)(2,1)S(1)} %collective-permute-done.16.c0_ref) | copy-start | bytes 1179652
  66.5 17.8 %collective-permute-start.11 = (bf16[2,4,2,16,1024]{4,3,2,1,0:T(8,128)(2,1)S(1)}, bf16[2,4,2,16,1024]{4,3,2,1,0:T(8,128)(2,1)S(1)}, u32[]{:S(2)}, u32[]{:S(2)}) collective-permute-start(bf16[2,4,2,16,1024]{4,3,2,1,0:T(8,128)(2,1)S(1)} %get-tuple-element.43), channel_id=1, source_target_pairs={{0,3},{1,0},{2,1},{3,2},{4,7},{5,4},{6,5},{7,6},{8,11},{9,8},{10,9... | collective-permute-start | bytes 1572872 | tf_op jit(solution)/shard_map/ppermute | solution.py:22
  66.5 8.9 %copy-start.9 = (bf16[2,4,16,1536]{3,2,1,0:T(8,128)(2,1)}, bf16[2,4,16,1536]{3,2,1,0:T(8,128)(2,1)S(1)}, u32[]{:S(2)}) copy-start(bf16[2,4,16,1536]{3,2,1,0:T(8,128)(2,1)S(1)} %collective-permute-done.17.c1_ref) | copy-start | bytes 1179652
  66.5 32.9 %collective-permute-start.5 = (bf16[2,4,2,16,1536]{4,3,2,1,0:T(8,128)(2,1)}, bf16[2,4,2,16,1536]{4,3,2,1,0:T(8,128)(2,1)S(1)}, u32[]{:S(2)}, u32[]{:S(2)}) collective-permute-start(bf16[2,4,2,16,1536]{4,3,2,1,0:T(8,128)(2,1)} %get-tuple-element.35), channel_id=1, source_target_pairs={{0,1},{1,2},{2,3},{3,0},{4,5},{5,6},{6,7},{7,4},{8,9},{9,10},{10,1... | collective-permute-start | bytes 2359304 | tf_op jit(solution)/shard_map/ppermute | solution.py:22
  71.7 6.3 %copy-start.10 = (bf16[2,4,16,1024]{3,2,1,0:T(8,128)(2,1)}, bf16[2,4,16,1024]{3,2,1,0:T(8,128)(2,1)S(1)}, u32[]{:S(2)}) copy-start(bf16[2,4,16,1024]{3,2,1,0:T(8,128)(2,1)S(1)} %collective-permute-done.12.xrc_ref) | copy-start | bytes 786436
  71.7 27.8 %collective-permute-start.6 = (bf16[2,4,2,16,1536]{4,3,2,1,0:T(8,128)(2,1)}, bf16[2,4,2,16,1536]{4,3,2,1,0:T(8,128)(2,1)S(1)}, u32[]{:S(2)}, u32[]{:S(2)}) collective-permute-start(bf16[2,4,2,16,1536]{4,3,2,1,0:T(8,128)(2,1)} %get-tuple-element.36), channel_id=1, source_target_pairs={{0,3},{1,0},{2,1},{3,2},{4,7},{5,4},{6,5},{7,6},{8,11},{9,8},{10,9... | collective-permute-start | bytes 2359304 | tf_op jit(solution)/shard_map/ppermute | solution.py:22
  75.4 24.1 %collective-permute-start.8 = (bf16[4,2,2,16,1536]{4,3,2,1,0:T(8,128)(2,1)}, bf16[4,2,2,16,1536]{4,3,2,1,0:T(8,128)(2,1)S(1)}, u32[]{:S(2)}, u32[]{:S(2)}) collective-permute-start(bf16[4,2,2,16,1536]{4,3,2,1,0:T(8,128)(2,1)} %get-tuple-element.39), channel_id=1, source_target_pairs={{0,120},{8,0},{16,8},{24,16},{32,24},{40,32},{48,40},{56,48},{64,5... | collective-permute-start | bytes 2359304 | tf_op jit(solution)/shard_map/ppermute | solution.py:22
  83.4 1.0 copy-start.4
  83.4 27.5 %collective-permute-start.18 = (bf16[2,4,2,16,1536]{4,3,2,1,0:T(8,128)(2,1)}, bf16[2,4,2,16,1536]{4,3,2,1,0:T(8,128)(2,1)S(1)}, u32[]{:S(2)}, u32[]{:S(2)}) collective-permute-start(bf16[2,4,2,16,1536]{4,3,2,1,0:T(8,128)(2,1)} %corner_sum.2), channel_id=1, source_target_pairs={{0,124},{4,120},{8,4},{12,0},{16,12},{20,8},{24,20},{28,16},{32,28... | collective-permute-start | bytes 2359304 | tf_op jit(solution)/shard_map/ppermute | solution.py:31
  84.4 0.8 copy-start.5
  95.9 11.7 %collective-permute-start.15 = (bf16[4,2,2,16,1024]{4,3,2,1,0:T(8,128)(2,1)}, bf16[4,2,2,16,1024]{4,3,2,1,0:T(8,128)(2,1)S(1)}, u32[]{:S(2)}, u32[]{:S(2)}) collective-permute-start(bf16[4,2,2,16,1024]{4,3,2,1,0:T(8,128)(2,1)} %get-tuple-element.51), channel_id=1, source_target_pairs={{0,120},{8,0},{16,8},{24,16},{32,24},{40,32},{48,40},{56,48},{64,5... | collective-permute-start | bytes 1572872 | tf_op jit(solution)/shard_map/ppermute | solution.py:22
  99.5 0.9 copy-start.2
  99.5 1.1 copy-start.3
  100.6 3.8 %copy-start.14 = (bf16[2,4,2,16,1024]{4,3,2,1,0:T(8,128)(2,1)S(1)}, bf16[2,4,2,16,1024]{4,3,2,1,0:T(8,128)(2,1)}, u32[]{:S(2)}) copy-start(bf16[2,4,2,16,1024]{4,3,2,1,0:T(8,128)(2,1)} %get-tuple-element.50) | copy-start | bytes 1572868
  100.6 10.3 %copy-start.15 = (bf16[2,4,16,1024]{3,2,1,0:T(8,128)(2,1)S(1)}, bf16[2,4,16,1024]{3,2,1,0:T(8,128)(2,1)}, u32[]{:S(2)}) copy-start(bf16[2,4,16,1024]{3,2,1,0:T(8,128)(2,1)} %get-tuple-element.64) | copy-start | bytes 786436
  104.4 16.3 %collective-permute-start.13 = (bf16[2,4,2,16,1024]{4,3,2,1,0:T(8,128)(2,1)}, bf16[2,4,2,16,1024]{4,3,2,1,0:T(8,128)(2,1)S(1)}, u32[]{:S(2)}, u32[]{:S(2)}) collective-permute-start(bf16[2,4,2,16,1024]{4,3,2,1,0:T(8,128)(2,1)} %get-tuple-element.49), channel_id=1, source_target_pairs={{0,1},{1,2},{2,3},{3,0},{4,5},{5,6},{6,7},{7,4},{8,9},{9,10},{10,1... | collective-permute-start | bytes 1572872 | tf_op jit(solution)/shard_map/ppermute | solution.py:22
  104.4 16.3 %collective-permute-start.14 = (bf16[2,4,2,16,1024]{4,3,2,1,0:T(8,128)(2,1)S(1)}, bf16[2,4,2,16,1024]{4,3,2,1,0:T(8,128)(2,1)S(1)}, u32[]{:S(2)}, u32[]{:S(2)}) collective-permute-start(bf16[2,4,2,16,1024]{4,3,2,1,0:T(8,128)(2,1)S(1)} %copy-done.14), channel_id=1, source_target_pairs={{0,3},{1,0},{2,1},{3,2},{4,7},{5,4},{6,5},{7,6},{8,11},{9,8},{10,9... | collective-permute-start | bytes 1572872 | tf_op jit(solution)/shard_map/ppermute | solution.py:22
  107.7 43.7 %collective-permute-start.19 = (bf16[2,4,2,2,16,1536]{5,4,3,2,1,0:T(8,128)(2,1)}, bf16[2,4,2,2,16,1536]{5,4,3,2,1,0:T(8,128)(2,1)S(1)}, u32[]{:S(2)}, u32[]{:S(2)}) collective-permute-start(bf16[2,4,2,2,16,1536]{5,4,3,2,1,0:T(8,128)(2,1)} %own_sum.2), channel_id=1, source_target_pairs={{0,120},{8,0},{16,8},{24,16},{32,24},{40,32},{48,40},{56,48},{64,5... | collective-permute-start | bytes 4718600 | tf_op jit(solution)/shard_map/ppermute | solution.py:22
  107.7 17.2 %collective-permute-start.21 = (bf16[2,4,16,1024]{3,2,1,0:T(8,128)(2,1)}, bf16[2,4,16,1024]{3,2,1,0:T(8,128)(2,1)S(1)}, u32[]{:S(2)}, u32[]{:S(2)}) collective-permute-start(bf16[2,4,16,1024]{3,2,1,0:T(8,128)(2,1)} %get-tuple-element.63), channel_id=1, source_target_pairs={{0,1},{1,2},{2,3},{3,0},{4,5},{5,6},{6,7},{7,4},{8,9},{9,10},{10,1... | collective-permute-start | bytes 786440 | tf_op jit(solution)/shard_map/ppermute | solution.py:22
  110.9 13.9 %collective-permute-start.22 = (bf16[2,4,16,1024]{3,2,1,0:T(8,128)(2,1)S(1)}, bf16[2,4,16,1024]{3,2,1,0:T(8,128)(2,1)S(1)}, u32[]{:S(2)}, u32[]{:S(2)}) collective-permute-start(bf16[2,4,16,1024]{3,2,1,0:T(8,128)(2,1)S(1)} %copy-done.15), channel_id=1, source_target_pairs={{0,3},{1,0},{2,1},{3,2},{4,7},{5,4},{6,5},{7,6},{8,11},{9,8},{10,9... | collective-permute-start | bytes 786440 | tf_op jit(solution)/shard_map/ppermute | solution.py:22
  120.7 0.8 copy-start.6
  120.7 1.0 copy-start.7
  124.6 26.7 %collective-permute-start.20 = (bf16[2,4,2,2,16,1024]{5,4,3,2,1,0:T(8,128)(2,1)}, bf16[2,4,2,2,16,1024]{5,4,3,2,1,0:T(8,128)(2,1)S(1)}, u32[]{:S(2)}, u32[]{:S(2)}) collective-permute-start(bf16[2,4,2,2,16,1024]{5,4,3,2,1,0:T(8,128)(2,1)} %own_sum.3), channel_id=1, source_target_pairs={{0,120},{8,0},{16,8},{24,16},{32,24},{40,32},{48,40},{56,48},{64,5... | collective-permute-start | bytes 3145736 | tf_op jit(solution)/shard_map/ppermute | solution.py:22
  124.9 0.7 copy-start.11
  124.9 0.8 copy-start.12
  127.9 23.1 %collective-permute-start.23 = (bf16[2,4,2,16,1024]{4,3,2,1,0:T(8,128)(2,1)}, bf16[2,4,2,16,1024]{4,3,2,1,0:T(8,128)(2,1)S(1)}, u32[]{:S(2)}, u32[]{:S(2)}) collective-permute-start(bf16[2,4,2,16,1024]{4,3,2,1,0:T(8,128)(2,1)} %corner_sum.3), channel_id=1, source_target_pairs={{0,124},{4,120},{8,4},{12,0},{16,12},{20,8},{24,20},{28,16},{32,28... | collective-permute-start | bytes 1572872 | tf_op jit(solution)/shard_map/ppermute | solution.py:31
where the time goes:
time: 155 us
  waiting for transfers between devices  70.7 us (46%)
  Pallas kernels  36.8 us (24%)
  starting transfers between devices  32.2 us (21%)
  local copies, waits for them, and re-layouts  10.5 us (7%)
  other arithmetic  4.15 us (3%)
    ppermute x22, waiting for transfers between devices, shift(): lax.ppermute(block, axis, [(i, (i + step) % count) for i in range(count)])  45.3 us
    ppermute x22, starting transfers between devices, shift(): lax.ppermute(block, axis, [(i, (i + step) % count) for i in range(count)])  31.4 us
    ppermute x2, waiting for transfers between devices, shift_across(): return lax.ppermute(block, ('section', 'ha'), route)  25.5 us
    pallas_call x2, Pallas kernels, local(): call(functools.partial(attend, base), [SMEM, SMEM] + [VMEM] * 8, [sd((tim...  25.1 us
    pallas_call x2, Pallas kernels, local(): call(own_sum, [VMEM] * 3, sd((2, times, 2, 2, tok, width), BF), 'own_sum'...  6.79 us
    pallas_call x2, Pallas kernels, local(): call(corner_sum, [VMEM] * 3, sd((2, *body), BF), 'corner_sum', moved=4 *...  4.83 us
    unnamed x34, local copies, waits for them, and re-layouts  4.62 us
  transfers between devices with their start and end apart: 24, of which 10 were waited for; matrix products, arithmetic and copies ran while one was open for 4% of the time, Pallas kernels for 24%

commit v1 on v0

--- a/solution.py
+++ b/solution.py
@@ -12,7 +12,7 @@
 LOG2E = 1.4426950408889634
 CHUNKS = (12, 8)
 NEG = -1e30
-GROUP = 2
+GROUP = 4
 BF = jnp.bfloat16
 F32 = jnp.float32
 
@@ -170,11 +170,12 @@
     def step(index, carry):
         each = [index * GROUP + i for i in range(GROUP)]
         loaded = [load(i) for i in each]
-        made = [products(x) for x in loaded]
-        soft = [soften(x) for x in made]
-        done = [gradients(x, y) for x, y in zip(loaded, soft)]
-        for i, d in zip(each, done):
-            store(pl.ds(pl.multiple_of(i * HEAD_DIM, HEAD_DIM), HEAD_DIM), d)
+        made = [products(loaded[0])]
+        for n, i in enumerate(each):
+            if n + 1 < GROUP:
+                made.append(products(loaded[n + 1]))
+            done = gradients(loaded[n], soften(made[n]))
+            store(pl.ds(pl.multiple_of(i * HEAD_DIM, HEAD_DIM), HEAD_DIM), done)
         return carry
 
     lax.fori_loop(0, heads // GROUP, step, 0)
@@ -188,7 +189,7 @@
 def own_sum(own_ref, r0_ref, r1_ref, out_ref):
     for s in range(2):
         for j, ref in enumerate((r0_ref, r1_ref)):
-            out_ref[s, :, :, j] = (own_ref[s, :, :, j] + ref[s].astype(F32)).astype(BF)
+            out_ref[s, :, :, j] = (own_ref[s, :, :, j].astype(F32) + ref[s].astype(F32)).astype(BF)
 
 
 VMEM = pl.BlockSpec(memory_space=pltpu.VMEM)
@@ -256,7 +257,7 @@
             [SMEM, SMEM] + [VMEM] * 8,
             [
                 sd((times, 2, 2, tok, width), BF),
-                sd((2, times, 2, 2, tok, width), F32),
+                sd((2, times, 2, 2, tok, width), BF),
                 sd((2, *body), F32),
                 sd((2, *body), BF),
                 sd((2, times, tok, width), BF),

time: 155 us -> 153 us (0.987)
  Pallas kernels: 36.8 us -> 34.2 us
    pallas_call x2, Pallas kernels: 25.1 us -> 23.2 us  [local(): call(functools.partial(attend, base), [SMEM, SMEM] + [VMEM] * 8, [sd((tim...]
  transfers between devices with their start and end apart: 24 -> 24, of which waited for: 10 -> 10; matrix products, arithmetic and copies ran while one was open for 4% -> 4% of each run, Pallas kernels for 24% -> 22%
where the time goes in v1:
time: 153 us; the launch traced here: 152 us
  waiting for transfers between devices  70.4 us (46%)
  Pallas kernels  34.2 us (22%)
  starting transfers between devices  32.7 us (21%)
  local copies, waits for them, and re-layouts  10.7 us (7%)
  other arithmetic  4.19 us (3%)
    ppermute x22, waiting for transfers between devices, shift(): lax.ppermute(block, axis, [(i, (i + step) % count) for i in range(count)])  44.4 us
    ppermute x22, starting transfers between devices, shift(): lax.ppermute(block, axis, [(i, (i + step) % count) for i in range(count)])  31.5 us
    ppermute x2, waiting for transfers between devices, shift_across(): return lax.ppermute(block, ('section', 'ha'), route)  26.1 us
    pallas_call x2, Pallas kernels, local(): call(functools.partial(attend, base), [SMEM, SMEM] + [VMEM] * 8, [sd((tim...  23.2 us
    pallas_call x2, Pallas kernels, local(): call(own_sum, [VMEM] * 3, sd((2, times, 2, 2, tok, width), BF), 'own_sum'...  6.09 us
    pallas_call x2, Pallas kernels, local(): call(corner_sum, [VMEM] * 3, sd((2, *body), BF), 'corner_sum', moved=4 *...  4.84 us
    unnamed x34, local copies, waits for them, and re-layouts  4.74 us
  transfers between devices with their start and end apart: 24, of which 10 were waited for; matrix products, arithmetic and copies ran while one was open for 4% of the time, Pallas kernels for 22%

profile of v1, /device:TPU:6, one launch (start us, length us, event | category | flops | bytes accessed | tf_op | source)
XLA Modules:
  0.0 152.4 jit_solution(12601851745535797107)
XLA Ops:
  0.0 1.6 %copy_bitcast_fusion.1 = bf16[2,4,2,16,2560]{4,3,1,0,2:T(8,128)(2,1)S(1)} fusion(bf16[2,1,4,2,2,16,2560]{6,5,4,3,2,1,0:T(8,128)(2,1)} %param.5, s32[]{:T(128)S(6)} %select_n.8), kind=kLoop, calls=%fused_computation.5 | loop fusion | bytes 2621444 | tf_op jit(solution)/shard_map/jit(dynamic_index_in_dim)/squeeze | solution.py:219
  1.6 4.0 %collective-permute-start = (bf16[2,4,2,16,1536]{4,3,1,0,2:T(8,128)(2,1)S(1)}, bf16[2,4,2,16,1536]{4,3,1,0,2:T(8,128)(2,1)S(1)}, u32[]{:S(2)}, u32[]{:S(2)}) collective-permute-start(bf16[2,4,2,16,1536]{4,3,1,0,2:T(8,128)(2,1)S(1)} %slice.40), channel_id=1, source_target_pairs={{0,4},{4,0},{1,5},{5,1},{2,6},{6,2},{3,7},{7,3},{8,12},{12,8},{9,1... | collective-permute-start | bytes 2359304 | tf_op jit(solution)/shard_map/ppermute | solution.py:22
  5.6 0.2 copy.17
  5.8 0.1 slice_bitcast_fusion
  5.9 3.1 %collective-permute-start.3 = (bf16[2,4,2,16,1536]{4,3,2,1,0:T(8,128)(2,1)S(1)}, bf16[2,4,2,16,1536]{4,3,2,1,0:T(8,128)(2,1)}, u32[]{:S(2)}, u32[]{:S(2)}) collective-permute-start(bf16[2,4,2,16,1536]{4,3,2,1,0:T(8,128)(2,1)S(1)} %get-tuple-element.67), channel_id=1, source_target_pairs={{0,3},{1,0},{2,1},{3,2},{4,7},{5,4},{6,5},{7,6},{8,11},{9,8},{10,9... | collective-permute-start | bytes 2359304 | tf_op jit(solution)/shard_map/ppermute | solution.py:22
  9.0 14.1 %collective-permute-done = bf16[2,4,2,16,1536]{4,3,1,0,2:T(8,128)(2,1)S(1)} collective-permute-done((bf16[2,4,2,16,1536]{4,3,1,0,2:T(8,128)(2,1)S(1)}, bf16[2,4,2,16,1536]{4,3,1,0,2:T(8,128)(2,1)S(1)}, u32[]{:S(2)}, u32[]{:S(2)}) %collective-permute-start) | collective-permute-done | bytes 786464 | tf_op jit(solution)/shard_map/ppermute | solution.py:22
  23.1 0.9 slice_bitcast_fusion.4
  24.1 3.0 %collective-permute-start.4 = (bf16[2,4,16,1536]{3,2,1,0:T(8,128)(2,1)}, bf16[2,4,16,1536]{3,2,1,0:T(8,128)(2,1)}, u32[]{:S(2)}, u32[]{:S(2)}) collective-permute-start(bf16[2,4,16,1536]{3,2,1,0:T(8,128)(2,1)} %get-tuple-element.69), channel_id=1, source_target_pairs={{0,3},{1,0},{2,1},{3,2},{4,7},{5,4},{6,5},{7,6},{8,11},{9,8},{10,9... | collective-permute-start | bytes 1179656 | tf_op jit(solution)/shard_map/ppermute | solution.py:22
  27.1 3.3 %collective-permute-start.7 = (bf16[2,4,2,16,1024]{4,3,1,0,2:T(8,128)(2,1)S(1)}, bf16[2,4,2,16,1024]{4,3,1,0,2:T(8,128)(2,1)S(1)}, u32[]{:S(2)}, u32[]{:S(2)}) collective-permute-start(bf16[2,4,2,16,1024]{4,3,1,0,2:T(8,128)(2,1)S(1)} %slice.45), channel_id=1, source_target_pairs={{0,4},{4,0},{1,5},{5,1},{2,6},{6,2},{3,7},{7,3},{8,12},{12,8},{9,1... | collective-permute-start | bytes 1572872 | tf_op jit(solution)/shard_map/ppermute | solution.py:22
  30.5 0.7 copy.7.starts_ref
  31.1 0.7 pad_add_fusion.place_ref
  31.8 1.0 copy.9.z_ref
  32.8 2.4 %collective-permute-done.4.xrc_ref = bf16[2,4,16,1536]{3,2,1,0:T(8,128)(2,1)} collective-permute-done((bf16[2,4,16,1536]{3,2,1,0:T(8,128)(2,1)}, bf16[2,4,16,1536]{3,2,1,0:T(8,128)(2,1)}, u32[]{:S(2)}, u32[]{:S(2)}) %collective-permute-start.4) | collective-permute-done | bytes 393248 | tf_op jit(solution)/shard_map/ppermute | solution.py:22
  35.2 3.4 %collective-permute-done.2.xlc_ref = bf16[2,4,16,1536]{3,2,1,0:T(8,128)(2,1)} collective-permute-done((bf16[2,4,16,1536]{3,2,1,0:T(8,128)(2,1)}, bf16[2,4,16,1536]{3,2,1,0:T(8,128)(2,1)}, u32[]{:S(2)}, u32[]{:S(2)}) %collective-permute-start.2) | collective-permute-done | bytes 393248 | tf_op jit(solution)/shard_map/ppermute | solution.py:22
  38.6 13.3 %attend.2 = (bf16[4,2,2,16,1536]{4,3,2,1,0:T(8,128)(2,1)}, bf16[2,4,2,2,16,1536]{5,4,3,2,1,0:T(8,128)(2,1)}, f32[2,4,2,16,1536]{4,3,2,1,0:T(8,128)}, bf16[2,4,2,...) custom-call(s32[2]{0:T(128)} %pad_add_fusion.place_ref, ...), custom_call_target="tpu_custom_call" | custom-call | flops 2400000000 | bytes 12582912 | tf_op jit(solution)/shard_map/attend/pallas_call | solution.py:255
  52.0 3.2 %collective-permute-start.17 = (bf16[2,4,16,1536]{3,2,1,0:T(8,128)(2,1)}, bf16[2,4,16,1536]{3,2,1,0:T(8,128)(2,1)S(1)}, u32[]{:S(2)}, u32[]{:S(2)}) collective-permute-start(bf16[2,4,16,1536]{3,2,1,0:T(8,128)(2,1)} %get-tuple-element.54), channel_id=1, source_target_pairs={{0,3},{1,0},{2,1},{3,2},{4,7},{5,4},{6,5},{7,6},{8,11},{9,8},{10,9... | collective-permute-start | bytes 1179656 | tf_op jit(solution)/shard_map/ppermute | solution.py:22
  55.3 2.0 %collective-permute-start.10 = (bf16[2,4,16,1024]{3,2,1,0:T(8,128)(2,1)S(1)}, bf16[2,4,16,1024]{3,2,1,0:T(8,128)(2,1)}, u32[]{:S(2)}, u32[]{:S(2)}) collective-permute-start(bf16[2,4,16,1024]{3,2,1,0:T(8,128)(2,1)S(1)} %get-tuple-element.72), channel_id=1, source_target_pairs={{0,1},{1,2},{2,3},{3,0},{4,5},{5,6},{6,7},{7,4},{8,9},{9,10},{10,1... | collective-permute-start | bytes 786440 | tf_op jit(solution)/shard_map/ppermute | solution.py:22
  57.4 1.3 slice_bitcast_fusion.2
  58.7 6.7 %collective-permute-done.16.c0_ref = bf16[2,4,16,1536]{3,2,1,0:T(8,128)(2,1)S(1)} collective-permute-done((bf16[2,4,16,1536]{3,2,1,0:T(8,128)(2,1)}, bf16[2,4,16,1536]{3,2,1,0:T(8,128)(2,1)S(1)}, u32[]{:S(2)}, u32[]{:S(2)}) %collective-permute-start.16) | collective-permute-done | bytes 393248 | tf_op jit(solution)/shard_map/ppermute | solution.py:22
  65.5 2.0 %collective-permute-start.5 = (bf16[2,4,2,16,1536]{4,3,2,1,0:T(8,128)(2,1)}, bf16[2,4,2,16,1536]{4,3,2,1,0:T(8,128)(2,1)S(1)}, u32[]{:S(2)}, u32[]{:S(2)}) collective-permute-start(bf16[2,4,2,16,1536]{4,3,2,1,0:T(8,128)(2,1)} %get-tuple-element.35), channel_id=1, source_target_pairs={{0,1},{1,2},{2,3},{3,0},{4,5},{5,6},{6,7},{7,4},{8,9},{9,10},{10,1... | collective-permute-start | bytes 2359304 | tf_op jit(solution)/shard_map/ppermute | solution.py:22
  67.5 3.1 %collective-permute-done.12.xrc_ref = bf16[2,4,16,1024]{3,2,1,0:T(8,128)(2,1)S(1)} collective-permute-done((bf16[2,4,16,1024]{3,2,1,0:T(8,128)(2,1)S(1)}, bf16[2,4,16,1024]{3,2,1,0:T(8,128)(2,1)S(1)}, u32[]{:S(2)}, u32[]{:S(2)}) %collective-permute-start.12) | collective-permute-done | bytes 262176 | tf_op jit(solution)/shard_map/ppermute | solution.py:22
  70.6 3.7 %collective-permute-start.6 = (bf16[2,4,2,16,1536]{4,3,2,1,0:T(8,128)(2,1)}, bf16[2,4,2,16,1536]{4,3,2,1,0:T(8,128)(2,1)S(1)}, u32[]{:S(2)}, u32[]{:S(2)}) collective-permute-start(bf16[2,4,2,16,1536]{4,3,2,1,0:T(8,128)(2,1)} %get-tuple-element.36), channel_id=1, source_target_pairs={{0,3},{1,0},{2,1},{3,2},{4,7},{5,4},{6,5},{7,6},{8,11},{9,8},{10,9... | collective-permute-start | bytes 2359304 | tf_op jit(solution)/shard_map/ppermute | solution.py:22
  74.3 2.6 %corner_sum.2 = bf16[2,4,2,16,1536]{4,3,2,1,0:T(8,128)(2,1)} custom-call(f32[2,4,2,16,1536]{4,3,2,1,0:T(8,128)} %get-tuple-element.52.dz_ref, bf16[2,4,16,1536]{3,2,1,0:T(8,128)(2,1)} %copy-done.8, bf16[2,4,16,1536]{3,2,1,0:T(8,128)(2,1)} %copy-done.9), custom_call_target="tpu_custom_call" | custom-call | bytes 4194304 | tf_op jit(solution)/shard_map/corner_sum/pallas_call | solution.py:286
  76.9 5.4 %collective-permute-done.9.xl_ref = bf16[2,4,2,16,1024]{4,3,2,1,0:T(8,128)(2,1)S(1)} collective-permute-done((bf16[2,4,2,16,1024]{4,3,2,1,0:T(8,128)(2,1)S(1)}, bf16[2,4,2,16,1024]{4,3,2,1,0:T(8,128)(2,1)S(1)}, u32[]{:S(2)}, u32[]{:S(2)}) %collective-permute-start.9) | collective-permute-done | bytes 524320 | tf_op jit(solution)/shard_map/ppermute | solution.py:22
  82.3 0.9 copy.12.z_ref
  83.2 0.1 copy-done.4
  83.3 0.8 copy-done.5
  84.1 10.0 %attend.3 = (bf16[4,2,2,16,1024]{4,3,2,1,0:T(8,128)(2,1)}, bf16[2,4,2,2,16,1024]{5,4,3,2,1,0:T(8,128)(2,1)}, f32[2,4,2,16,1024]{4,3,2,1,0:T(8,128)}, bf16[2,4,2,...) custom-call(s32[2]{0:T(128)} %pad_add_fusion.place_ref, ...), custom_call_target="tpu_custom_call" | custom-call | flops 1600000000 | bytes 8388608 | tf_op jit(solution)/shard_map/attend/pallas_call | solution.py:255
  94.1 3.7 %collective-permute-start.15 = (bf16[4,2,2,16,1024]{4,3,2,1,0:T(8,128)(2,1)}, bf16[4,2,2,16,1024]{4,3,2,1,0:T(8,128)(2,1)S(1)}, u32[]{:S(2)}, u32[]{:S(2)}) collective-permute-start(bf16[4,2,2,16,1024]{4,3,2,1,0:T(8,128)(2,1)} %get-tuple-element.51), channel_id=1, source_target_pairs={{0,120},{8,0},{16,8},{24,16},{32,24},{40,32},{48,40},{56,48},{64,5... | collective-permute-start | bytes 1572872 | tf_op jit(solution)/shard_map/ppermute | solution.py:22
  97.8 0.9 copy-done.2
  98.7 0.3 copy-done.3
  99.0 3.3 %own_sum.2 = bf16[2,4,2,2,16,1536]{5,4,3,2,1,0:T(8,128)(2,1)} custom-call(bf16[2,4,2,2,16,1536]{5,4,3,2,1,0:T(8,128)(2,1)} %get-tuple-element.46.own_ref, bf16[2,4,2,16,1536]{4,3,2,1,0:T(8,128)(2,1)} %copy-done.2, bf16[2,4,2,16,1536]{4,3,2,1,0:T(8,128)(2,1)} %copy-done.3), custom_call_target="tpu_custom_call" | custom-call | bytes 5242880 | tf_op jit(solution)/shard_map/own_sum/pallas_call | solution.py:292
  102.3 3.2 %collective-permute-start.14 = (bf16[2,4,2,16,1024]{4,3,2,1,0:T(8,128)(2,1)S(1)}, bf16[2,4,2,16,1024]{4,3,2,1,0:T(8,128)(2,1)S(1)}, u32[]{:S(2)}, u32[]{:S(2)}) collective-permute-start(bf16[2,4,2,16,1024]{4,3,2,1,0:T(8,128)(2,1)S(1)} %copy-done.14), channel_id=1, source_target_pairs={{0,3},{1,0},{2,1},{3,2},{4,7},{5,4},{6,5},{7,6},{8,11},{9,8},{10,9... | collective-permute-start | bytes 1572872 | tf_op jit(solution)/shard_map/ppermute | solution.py:22
  105.6 4.3 %collective-permute-done.18 = bf16[2,4,2,16,1536]{4,3,2,1,0:T(8,128)(2,1)S(1)} collective-permute-done((bf16[2,4,2,16,1536]{4,3,2,1,0:T(8,128)(2,1)}, bf16[2,4,2,16,1536]{4,3,2,1,0:T(8,128)(2,1)S(1)}, u32[]{:S(2)}, u32[]{:S(2)}) %collective-permute-start.18) | collective-permute-done | bytes 786464 | tf_op jit(solution)/shard_map/ppermute | solution.py:31
  109.8 8.7 %collective-permute-done.13.r0_ref = bf16[2,4,2,16,1024]{4,3,2,1,0:T(8,128)(2,1)S(1)} collective-permute-done((bf16[2,4,2,16,1024]{4,3,2,1,0:T(8,128)(2,1)}, bf16[2,4,2,16,1024]{4,3,2,1,0:T(8,128)(2,1)S(1)}, u32[]{:S(2)}, u32[]{:S(2)}) %collective-permute-start.13) | collective-permute-done | bytes 524320 | tf_op jit(solution)/shard_map/ppermute | solution.py:22
  118.6 0.8 copy-done.6
  119.4 0.2 copy-done.7
  119.6 2.8 %own_sum.3 = bf16[2,4,2,2,16,1024]{5,4,3,2,1,0:T(8,128)(2,1)} custom-call(bf16[2,4,2,2,16,1024]{5,4,3,2,1,0:T(8,128)(2,1)} %get-tuple-element.56.own_ref, bf16[2,4,2,16,1024]{4,3,2,1,0:T(8,128)(2,1)} %copy-done.6, bf16[2,4,2,16,1024]{4,3,2,1,0:T(8,128)(2,1)} %copy-done.7), custom_call_target="tpu_custom_call" | custom-call | bytes 5242880 | tf_op jit(solution)/shard_map/own_sum/pallas_call | solution.py:292
  122.3 0.4 collective-permute-done.21.c0_ref
  122.8 0.7 copy-done.11
  123.5 0.1 copy-done.12
  123.6 2.2 %corner_sum.3 = bf16[2,4,2,16,1024]{4,3,2,1,0:T(8,128)(2,1)} custom-call(f32[2,4,2,16,1024]{4,3,2,1,0:T(8,128)} %get-tuple-element.60.dz_ref, bf16[2,4,16,1024]{3,2,1,0:T(8,128)(2,1)} %copy-done.11, bf16[2,4,16,1024]{3,2,1,0:T(8,128)(2,1)} %copy-done.12), custom_call_target="tpu_custom_call" | custom-call | bytes 4194304 | tf_op jit(solution)/shard_map/corner_sum/pallas_call | solution.py:286
  125.8 1.2 collective-permute-start.23
  127.0 0.1 maximum_bitcast_fusion.1
  127.1 21.8 %collective-permute-done.23 = bf16[2,4,2,16,1024]{4,3,2,1,0:T(8,128)(2,1)S(1)} collective-permute-done((bf16[2,4,2,16,1024]{4,3,2,1,0:T(8,128)(2,1)}, bf16[2,4,2,16,1024]{4,3,2,1,0:T(8,128)(2,1)S(1)}, u32[]{:S(2)}, u32[]{:S(2)}) %collective-permute-start.23) | collective-permute-done | bytes 524320 | tf_op jit(solution)/shard_map/ppermute | solution.py:31
  148.9 0.3 maximum_convert_fusion
  149.2 0.9 add_convert_fusion
  150.1 2.3 %maximum_bitcast_fusion = bf16[3,1,4,2,2,16,2560]{6,5,4,3,2,1,0:T(8,128)(2,1)} fusion(bf16[2,4,2,2,16,2560]{5,4,3,2,1,0:T(8,128)(2,1)S(1)} %add_convert_fusion, bf16[1,4,2,2,16,2560]{5,4,3,2,1,0:T(8,128)(2,1)S(1)} %maximum_bitcast_fusion.1), kind=kLoop, calls=%fused_computation.1 | loop fusion | flops 1966080 | bytes 7864320 | tf_op jit(solution)/shard_map/broadcast_in_dim | solution.py:303
  (55 shorter events, 0.5 us)
Async XLA Ops:
  0.0 5.6 %copy-start = (bf16[2,1,4,2,2,16,2560]{6,5,4,3,2,1,0:T(8,128)(2,1)S(1)}, bf16[2,1,4,2,2,16,2560]{6,5,4,3,2,1,0:T(8,128)(2,1)}, u32[]{:S(2)}) copy-start(bf16[2,1,4,2,2,16,2560]{6,5,4,3,2,1,0:T(8,128)(2,1)} %param.5) | copy-start | bytes 7864324
  1.6 21.5 %collective-permute-start = (bf16[2,4,2,16,1536]{4,3,1,0,2:T(8,128)(2,1)S(1)}, bf16[2,4,2,16,1536]{4,3,1,0,2:T(8,128)(2,1)S(1)}, u32[]{:S(2)}, u32[]{:S(2)}) collective-permute-start(bf16[2,4,2,16,1536]{4,3,1,0,2:T(8,128)(2,1)S(1)} %slice.40), channel_id=1, source_target_pairs={{0,4},{4,0},{1,5},{5,1},{2,6},{6,2},{3,7},{7,3},{8,12},{12,8},{9,1... | collective-permute-start | bytes 2359304 | tf_op jit(solution)/shard_map/ppermute | solution.py:22
  5.8 21.4 %copy-start.1 = (bf16[2,1,4,2,2,16,2560]{6,5,3,2,0,4,1:T(8,128)(2,1)}, bf16[2,1,4,2,2,16,2560]{6,5,3,2,0,4,1:T(8,128)(2,1)S(1)}, u32[]{:S(2)}) copy-start(bf16[2,1,4,2,2,16,2560]{6,5,3,2,0,4,1:T(8,128)(2,1)S(1)} %copy.17) | copy-start | bytes 7864324
  5.8 24.7 %copy-start.13 = (s32[4,2,2]{0,2,1:T(2,128)S(1)}, s32[4,2,2]{0,2,1:T(2,128)}, u32[]{:S(2)}) copy-start(s32[4,2,2]{0,2,1:T(2,128)} %param.7) | copy-start | bytes 196
  5.9 26.9 %collective-permute-start.3 = (bf16[2,4,2,16,1536]{4,3,2,1,0:T(8,128)(2,1)S(1)}, bf16[2,4,2,16,1536]{4,3,2,1,0:T(8,128)(2,1)}, u32[]{:S(2)}, u32[]{:S(2)}) collective-permute-start(bf16[2,4,2,16,1536]{4,3,2,1,0:T(8,128)(2,1)S(1)} %get-tuple-element.67), channel_id=1, source_target_pairs={{0,3},{1,0},{2,1},{3,2},{4,7},{5,4},{6,5},{7,6},{8,11},{9,8},{10,9... | collective-permute-start | bytes 2359304 | tf_op jit(solution)/shard_map/ppermute | solution.py:22
  9.0 23.8 %collective-permute-start.1 = (bf16[2,4,2,16,1536]{4,3,2,1,0:T(8,128)(2,1)S(1)}, bf16[2,4,2,16,1536]{4,3,2,1,0:T(8,128)(2,1)}, u32[]{:S(2)}, u32[]{:S(2)}) collective-permute-start(bf16[2,4,2,16,1536]{4,3,2,1,0:T(8,128)(2,1)S(1)} %get-tuple-element.68), channel_id=1, source_target_pairs={{0,1},{1,2},{2,3},{3,0},{4,5},{5,6},{6,7},{7,4},{8,9},{9,10},{10,1... | collective-permute-start | bytes 2359304 | tf_op jit(solution)/shard_map/ppermute | solution.py:22
  24.1 11.2 %collective-permute-start.4 = (bf16[2,4,16,1536]{3,2,1,0:T(8,128)(2,1)}, bf16[2,4,16,1536]{3,2,1,0:T(8,128)(2,1)}, u32[]{:S(2)}, u32[]{:S(2)}) collective-permute-start(bf16[2,4,16,1536]{3,2,1,0:T(8,128)(2,1)} %get-tuple-element.69), channel_id=1, source_target_pairs={{0,3},{1,0},{2,1},{3,2},{4,7},{5,4},{6,5},{7,6},{8,11},{9,8},{10,9... | collective-permute-start | bytes 1179656 | tf_op jit(solution)/shard_map/ppermute | solution.py:22
  27.1 11.5 %collective-permute-start.2 = (bf16[2,4,16,1536]{3,2,1,0:T(8,128)(2,1)}, bf16[2,4,16,1536]{3,2,1,0:T(8,128)(2,1)}, u32[]{:S(2)}, u32[]{:S(2)}) collective-permute-start(bf16[2,4,16,1536]{3,2,1,0:T(8,128)(2,1)} %get-tuple-element.70), channel_id=1, source_target_pairs={{0,1},{1,2},{2,3},{3,0},{4,5},{5,6},{6,7},{7,4},{8,9},{9,10},{10,1... | collective-permute-start | bytes 1179656 | tf_op jit(solution)/shard_map/ppermute | solution.py:22
  27.1 28.1 %collective-permute-start.7 = (bf16[2,4,2,16,1024]{4,3,1,0,2:T(8,128)(2,1)S(1)}, bf16[2,4,2,16,1024]{4,3,1,0,2:T(8,128)(2,1)S(1)}, u32[]{:S(2)}, u32[]{:S(2)}) collective-permute-start(bf16[2,4,2,16,1024]{4,3,1,0,2:T(8,128)(2,1)S(1)} %slice.45), channel_id=1, source_target_pairs={{0,4},{4,0},{1,5},{5,1},{2,6},{6,2},{3,7},{7,3},{8,12},{12,8},{9,1... | collective-permute-start | bytes 1572872 | tf_op jit(solution)/shard_map/ppermute | solution.py:22
  51.9 13.5 %collective-permute-start.16 = (bf16[2,4,16,1536]{3,2,1,0:T(8,128)(2,1)}, bf16[2,4,16,1536]{3,2,1,0:T(8,128)(2,1)S(1)}, u32[]{:S(2)}, u32[]{:S(2)}) collective-permute-start(bf16[2,4,16,1536]{3,2,1,0:T(8,128)(2,1)} %get-tuple-element.53), channel_id=1, source_target_pairs={{0,1},{1,2},{2,3},{3,0},{4,5},{5,6},{6,7},{7,4},{8,9},{9,10},{10,1... | collective-permute-start | bytes 1179656 | tf_op jit(solution)/shard_map/ppermute | solution.py:22
  52.0 13.5 %collective-permute-start.17 = (bf16[2,4,16,1536]{3,2,1,0:T(8,128)(2,1)}, bf16[2,4,16,1536]{3,2,1,0:T(8,128)(2,1)S(1)}, u32[]{:S(2)}, u32[]{:S(2)}) collective-permute-start(bf16[2,4,16,1536]{3,2,1,0:T(8,128)(2,1)} %get-tuple-element.54), channel_id=1, source_target_pairs={{0,3},{1,0},{2,1},{3,2},{4,7},{5,4},{6,5},{7,6},{8,11},{9,8},{10,9... | collective-permute-start | bytes 1179656 | tf_op jit(solution)/shard_map/ppermute | solution.py:22
  55.3 15.3 %collective-permute-start.12 = (bf16[2,4,16,1024]{3,2,1,0:T(8,128)(2,1)S(1)}, bf16[2,4,16,1024]{3,2,1,0:T(8,128)(2,1)S(1)}, u32[]{:S(2)}, u32[]{:S(2)}) collective-permute-start(bf16[2,4,16,1024]{3,2,1,0:T(8,128)(2,1)S(1)} %get-tuple-element.71), channel_id=1, source_target_pairs={{0,3},{1,0},{2,1},{3,2},{4,7},{5,4},{6,5},{7,6},{8,11},{9,8},{10,9... | collective-permute-start | bytes 786440 | tf_op jit(solution)/shard_map/ppermute | solution.py:22
  55.3 19.0 %collective-permute-start.10 = (bf16[2,4,16,1024]{3,2,1,0:T(8,128)(2,1)S(1)}, bf16[2,4,16,1024]{3,2,1,0:T(8,128)(2,1)}, u32[]{:S(2)}, u32[]{:S(2)}) collective-permute-start(bf16[2,4,16,1024]{3,2,1,0:T(8,128)(2,1)S(1)} %get-tuple-element.72), channel_id=1, source_target_pairs={{0,1},{1,2},{2,3},{3,0},{4,5},{5,6},{6,7},{7,4},{8,9},{9,10},{10,1... | collective-permute-start | bytes 786440 | tf_op jit(solution)/shard_map/ppermute | solution.py:22
  58.6 23.7 %collective-permute-start.9 = (bf16[2,4,2,16,1024]{4,3,2,1,0:T(8,128)(2,1)S(1)}, bf16[2,4,2,16,1024]{4,3,2,1,0:T(8,128)(2,1)S(1)}, u32[]{:S(2)}, u32[]{:S(2)}) collective-permute-start(bf16[2,4,2,16,1024]{4,3,2,1,0:T(8,128)(2,1)S(1)} %get-tuple-element.42), channel_id=1, source_target_pairs={{0,1},{1,2},{2,3},{3,0},{4,5},{5,6},{6,7},{7,4},{8,9},{9,10},{10,1... | collective-permute-start | bytes 1572872 | tf_op jit(solution)/shard_map/ppermute | solution.py:22
  65.4 8.9 %copy-start.8 = (bf16[2,4,16,1536]{3,2,1,0:T(8,128)(2,1)}, bf16[2,4,16,1536]{3,2,1,0:T(8,128)(2,1)S(1)}, u32[]{:S(2)}) copy-start(bf16[2,4,16,1536]{3,2,1,0:T(8,128)(2,1)S(1)} %collective-permute-done.16.c0_ref) | copy-start | bytes 1179652
  65.4 17.8 %collective-permute-start.11 = (bf16[2,4,2,16,1024]{4,3,2,1,0:T(8,128)(2,1)S(1)}, bf16[2,4,2,16,1024]{4,3,2,1,0:T(8,128)(2,1)S(1)}, u32[]{:S(2)}, u32[]{:S(2)}) collective-permute-start(bf16[2,4,2,16,1024]{4,3,2,1,0:T(8,128)(2,1)S(1)} %get-tuple-element.43), channel_id=1, source_target_pairs={{0,3},{1,0},{2,1},{3,2},{4,7},{5,4},{6,5},{7,6},{8,11},{9,8},{10,9... | collective-permute-start | bytes 1572872 | tf_op jit(solution)/shard_map/ppermute | solution.py:22
  65.5 8.9 %copy-start.9 = (bf16[2,4,16,1536]{3,2,1,0:T(8,128)(2,1)}, bf16[2,4,16,1536]{3,2,1,0:T(8,128)(2,1)S(1)}, u32[]{:S(2)}) copy-start(bf16[2,4,16,1536]{3,2,1,0:T(8,128)(2,1)S(1)} %collective-permute-done.17.c1_ref) | copy-start | bytes 1179652
  65.5 32.3 %collective-permute-start.5 = (bf16[2,4,2,16,1536]{4,3,2,1,0:T(8,128)(2,1)}, bf16[2,4,2,16,1536]{4,3,2,1,0:T(8,128)(2,1)S(1)}, u32[]{:S(2)}, u32[]{:S(2)}) collective-permute-start(bf16[2,4,2,16,1536]{4,3,2,1,0:T(8,128)(2,1)} %get-tuple-element.35), channel_id=1, source_target_pairs={{0,1},{1,2},{2,3},{3,0},{4,5},{5,6},{6,7},{7,4},{8,9},{9,10},{10,1... | collective-permute-start | bytes 2359304 | tf_op jit(solution)/shard_map/ppermute | solution.py:22
  70.6 6.3 %copy-start.10 = (bf16[2,4,16,1024]{3,2,1,0:T(8,128)(2,1)}, bf16[2,4,16,1024]{3,2,1,0:T(8,128)(2,1)S(1)}, u32[]{:S(2)}) copy-start(bf16[2,4,16,1024]{3,2,1,0:T(8,128)(2,1)S(1)} %collective-permute-done.12.xrc_ref) | copy-start | bytes 786436
  70.6 27.2 %collective-permute-start.6 = (bf16[2,4,2,16,1536]{4,3,2,1,0:T(8,128)(2,1)}, bf16[2,4,2,16,1536]{4,3,2,1,0:T(8,128)(2,1)S(1)}, u32[]{:S(2)}, u32[]{:S(2)}) collective-permute-start(bf16[2,4,2,16,1536]{4,3,2,1,0:T(8,128)(2,1)} %get-tuple-element.36), channel_id=1, source_target_pairs={{0,3},{1,0},{2,1},{3,2},{4,7},{5,4},{6,5},{7,6},{8,11},{9,8},{10,9... | collective-permute-start | bytes 2359304 | tf_op jit(solution)/shard_map/ppermute | solution.py:22
  74.3 23.5 %collective-permute-start.8 = (bf16[4,2,2,16,1536]{4,3,2,1,0:T(8,128)(2,1)}, bf16[4,2,2,16,1536]{4,3,2,1,0:T(8,128)(2,1)S(1)}, u32[]{:S(2)}, u32[]{:S(2)}) collective-permute-start(bf16[4,2,2,16,1536]{4,3,2,1,0:T(8,128)(2,1)} %get-tuple-element.39), channel_id=1, source_target_pairs={{0,120},{8,0},{16,8},{24,16},{32,24},{40,32},{48,40},{56,48},{64,5... | collective-permute-start | bytes 2359304 | tf_op jit(solution)/shard_map/ppermute | solution.py:22
  82.3 1.0 copy-start.4
  82.3 27.5 %collective-permute-start.18 = (bf16[2,4,2,16,1536]{4,3,2,1,0:T(8,128)(2,1)}, bf16[2,4,2,16,1536]{4,3,2,1,0:T(8,128)(2,1)S(1)}, u32[]{:S(2)}, u32[]{:S(2)}) collective-permute-start(bf16[2,4,2,16,1536]{4,3,2,1,0:T(8,128)(2,1)} %corner_sum.2), channel_id=1, source_target_pairs={{0,124},{4,120},{8,4},{12,0},{16,12},{20,8},{24,20},{28,16},{32,28... | collective-permute-start | bytes 2359304 | tf_op jit(solution)/shard_map/ppermute | solution.py:31
  83.3 0.8 copy-start.5
  94.1 8.2 %copy-start.14 = (bf16[2,4,2,16,1024]{4,3,2,1,0:T(8,128)(2,1)S(1)}, bf16[2,4,2,16,1024]{4,3,2,1,0:T(8,128)(2,1)}, u32[]{:S(2)}) copy-start(bf16[2,4,2,16,1024]{4,3,2,1,0:T(8,128)(2,1)} %get-tuple-element.50) | copy-start | bytes 1572868
  94.1 15.7 %copy-start.15 = (bf16[2,4,16,1024]{3,2,1,0:T(8,128)(2,1)S(1)}, bf16[2,4,16,1024]{3,2,1,0:T(8,128)(2,1)}, u32[]{:S(2)}) copy-start(bf16[2,4,16,1024]{3,2,1,0:T(8,128)(2,1)} %get-tuple-element.64) | copy-start | bytes 786436
  94.1 11.4 %collective-permute-start.15 = (bf16[4,2,2,16,1024]{4,3,2,1,0:T(8,128)(2,1)}, bf16[4,2,2,16,1024]{4,3,2,1,0:T(8,128)(2,1)S(1)}, u32[]{:S(2)}, u32[]{:S(2)}) collective-permute-start(bf16[4,2,2,16,1024]{4,3,2,1,0:T(8,128)(2,1)} %get-tuple-element.51), channel_id=1, source_target_pairs={{0,120},{8,0},{16,8},{24,16},{32,24},{40,32},{48,40},{56,48},{64,5... | collective-permute-start | bytes 1572872 | tf_op jit(solution)/shard_map/ppermute | solution.py:22
  97.8 0.9 copy-start.2
  97.8 1.2 copy-start.3
  102.3 16.3 %collective-permute-start.13 = (bf16[2,4,2,16,1024]{4,3,2,1,0:T(8,128)(2,1)}, bf16[2,4,2,16,1024]{4,3,2,1,0:T(8,128)(2,1)S(1)}, u32[]{:S(2)}, u32[]{:S(2)}) collective-permute-start(bf16[2,4,2,16,1024]{4,3,2,1,0:T(8,128)(2,1)} %get-tuple-element.49), channel_id=1, source_target_pairs={{0,1},{1,2},{2,3},{3,0},{4,5},{5,6},{6,7},{7,4},{8,9},{9,10},{10,1... | collective-permute-start | bytes 1572872 | tf_op jit(solution)/shard_map/ppermute | solution.py:22
  102.3 16.3 %collective-permute-start.14 = (bf16[2,4,2,16,1024]{4,3,2,1,0:T(8,128)(2,1)S(1)}, bf16[2,4,2,16,1024]{4,3,2,1,0:T(8,128)(2,1)S(1)}, u32[]{:S(2)}, u32[]{:S(2)}) collective-permute-start(bf16[2,4,2,16,1024]{4,3,2,1,0:T(8,128)(2,1)S(1)} %copy-done.14), channel_id=1, source_target_pairs={{0,3},{1,0},{2,1},{3,2},{4,7},{5,4},{6,5},{7,6},{8,11},{9,8},{10,9... | collective-permute-start | bytes 1572872 | tf_op jit(solution)/shard_map/ppermute | solution.py:22
  105.5 43.7 %collective-permute-start.19 = (bf16[2,4,2,2,16,1536]{5,4,3,2,1,0:T(8,128)(2,1)}, bf16[2,4,2,2,16,1536]{5,4,3,2,1,0:T(8,128)(2,1)S(1)}, u32[]{:S(2)}, u32[]{:S(2)}) collective-permute-start(bf16[2,4,2,2,16,1536]{5,4,3,2,1,0:T(8,128)(2,1)} %own_sum.2), channel_id=1, source_target_pairs={{0,120},{8,0},{16,8},{24,16},{32,24},{40,32},{48,40},{56,48},{64,5... | collective-permute-start | bytes 4718600 | tf_op jit(solution)/shard_map/ppermute | solution.py:22
  105.5 17.2 %collective-permute-start.21 = (bf16[2,4,16,1024]{3,2,1,0:T(8,128)(2,1)}, bf16[2,4,16,1024]{3,2,1,0:T(8,128)(2,1)S(1)}, u32[]{:S(2)}, u32[]{:S(2)}) collective-permute-start(bf16[2,4,16,1024]{3,2,1,0:T(8,128)(2,1)} %get-tuple-element.63), channel_id=1, source_target_pairs={{0,1},{1,2},{2,3},{3,0},{4,5},{5,6},{6,7},{7,4},{8,9},{9,10},{10,1... | collective-permute-start | bytes 786440 | tf_op jit(solution)/shard_map/ppermute | solution.py:22
  109.8 12.9 %collective-permute-start.22 = (bf16[2,4,16,1024]{3,2,1,0:T(8,128)(2,1)S(1)}, bf16[2,4,16,1024]{3,2,1,0:T(8,128)(2,1)S(1)}, u32[]{:S(2)}, u32[]{:S(2)}) collective-permute-start(bf16[2,4,16,1024]{3,2,1,0:T(8,128)(2,1)S(1)} %copy-done.15), channel_id=1, source_target_pairs={{0,3},{1,0},{2,1},{3,2},{4,7},{5,4},{6,5},{7,6},{8,11},{9,8},{10,9... | collective-permute-start | bytes 786440 | tf_op jit(solution)/shard_map/ppermute | solution.py:22
  118.6 0.8 copy-start.6
  118.6 1.0 copy-start.7
  122.3 26.9 %collective-permute-start.20 = (bf16[2,4,2,2,16,1024]{5,4,3,2,1,0:T(8,128)(2,1)}, bf16[2,4,2,2,16,1024]{5,4,3,2,1,0:T(8,128)(2,1)S(1)}, u32[]{:S(2)}, u32[]{:S(2)}) collective-permute-start(bf16[2,4,2,2,16,1024]{5,4,3,2,1,0:T(8,128)(2,1)} %own_sum.3), channel_id=1, source_target_pairs={{0,120},{8,0},{16,8},{24,16},{32,24},{40,32},{48,40},{56,48},{64,5... | collective-permute-start | bytes 3145736 | tf_op jit(solution)/shard_map/ppermute | solution.py:22
  122.7 0.7 copy-start.11
  122.8 0.8 copy-start.12
  125.8 23.1 %collective-permute-start.23 = (bf16[2,4,2,16,1024]{4,3,2,1,0:T(8,128)(2,1)}, bf16[2,4,2,16,1024]{4,3,2,1,0:T(8,128)(2,1)S(1)}, u32[]{:S(2)}, u32[]{:S(2)}) collective-permute-start(bf16[2,4,2,16,1024]{4,3,2,1,0:T(8,128)(2,1)} %corner_sum.3), channel_id=1, source_target_pairs={{0,124},{4,120},{8,4},{12,0},{16,12},{20,8},{24,20},{28,16},{32,28... | collective-permute-start | bytes 1572872 | tf_op jit(solution)/shard_map/ppermute | solution.py:31

commit v2 on v1

--- a/solution.py
+++ b/solution.py
@@ -159,7 +159,7 @@
             own_ref[s, :, :, :, :, cols] = (
                 d_own[s][:n_kv].reshape(times, 2, 2, tok, HEAD_DIM).astype(own_ref.dtype)
             )
-            dz_ref[s, :, :, :, cols] = d_own[s][n_kv:].reshape(times, 2, tok, HEAD_DIM)
+            dz_ref[s, :, :, :, cols] = d_own[s][n_kv:].reshape(times, 2, tok, HEAD_DIM).astype(BF)
             d0, d1 = d_x[s]
             left = (jnp.where(first, 0.0, d0) + jnp.where(last, d1, 0.0)).astype(BF)
             right = (jnp.where(last, 0.0, d1) + jnp.where(first, d0, 0.0)).astype(BF)
@@ -183,7 +183,7 @@
 
 def corner_sum(dz_ref, c0_ref, c1_ref, out_ref):
     for j, ref in enumerate((c0_ref, c1_ref)):
-        out_ref[:, :, j] = (dz_ref[:, :, j] + ref[...].astype(F32)).astype(BF)
+        out_ref[:, :, j] = (dz_ref[:, :, j].astype(F32) + ref[...].astype(F32)).astype(BF)
 
 
 def own_sum(own_ref, r0_ref, r1_ref, out_ref):
@@ -258,7 +258,7 @@
             [
                 sd((times, 2, 2, tok, width), BF),
                 sd((2, times, 2, 2, tok, width), BF),
-                sd((2, *body), F32),
+                sd((2, *body), BF),
                 sd((2, *body), BF),
                 sd((2, times, tok, width), BF),
                 sd((2, *body), BF),

time: 153 us -> 152 us (level)
  no operation moved by 1% of the time
where the time goes in v2:
time: 152 us
  waiting for transfers between devices  70.8 us (47%)
  Pallas kernels  33.8 us (22%)
  starting transfers between devices  32.7 us (22%)
  local copies, waits for them, and re-layouts  10.5 us (7%)
  other arithmetic  4.13 us (3%)
    ppermute x22, waiting for transfers between devices, shift(): lax.ppermute(block, axis, [(i, (i + step) % count) for i in range(count)])  44.6 us
    ppermute x22, starting transfers between devices, shift(): lax.ppermute(block, axis, [(i, (i + step) % count) for i in range(count)])  31.4 us
    ppermute x2, waiting for transfers between devices, shift_across(): return lax.ppermute(block, ('section', 'ha'), route)  26.3 us
    pallas_call x2, Pallas kernels, local(): call(functools.partial(attend, base), [SMEM, SMEM] + [VMEM] * 8, [sd((tim...  23.2 us
    pallas_call x2, Pallas kernels, local(): call(own_sum, [VMEM] * 3, sd((2, times, 2, 2, tok, width), BF), 'own_sum'...  6.09 us
    unnamed x34, local copies, waits for them, and re-layouts  4.69 us
    pallas_call x2, Pallas kernels, local(): call(corner_sum, [VMEM] * 3, sd((2, *body), BF), 'corner_sum', moved=4 *...  4.52 us
  transfers between devices with their start and end apart: 24, of which 10 were waited for; matrix products, arithmetic and copies ran while one was open for 4% of the time, Pallas kernels for 22%

profile of v2, /device:TPU:6, one launch (start us, length us, event | category | flops | bytes accessed | tf_op | source)
XLA Modules:
  0.0 152.2 jit_solution(10543763489491227677)
XLA Ops:
  0.0 1.6 %copy_bitcast_fusion.1 = bf16[2,4,2,16,2560]{4,3,1,0,2:T(8,128)(2,1)S(1)} fusion(bf16[2,1,4,2,2,16,2560]{6,5,4,3,2,1,0:T(8,128)(2,1)} %param.5, s32[]{:T(128)S(6)} %select_n.8), kind=kLoop, calls=%fused_computation.5 | loop fusion | bytes 2621444 | tf_op jit(solution)/shard_map/jit(dynamic_index_in_dim)/squeeze | solution.py:219
  1.6 4.0 %collective-permute-start = (bf16[2,4,2,16,1536]{4,3,1,0,2:T(8,128)(2,1)S(1)}, bf16[2,4,2,16,1536]{4,3,1,0,2:T(8,128)(2,1)S(1)}, u32[]{:S(2)}, u32[]{:S(2)}) collective-permute-start(bf16[2,4,2,16,1536]{4,3,1,0,2:T(8,128)(2,1)S(1)} %slice.40), channel_id=1, source_target_pairs={{0,4},{4,0},{1,5},{5,1},{2,6},{6,2},{3,7},{7,3},{8,12},{12,8},{9,1... | collective-permute-start | bytes 2359304 | tf_op jit(solution)/shard_map/ppermute | solution.py:22
  5.6 0.2 copy.17
  5.8 0.1 slice_bitcast_fusion
  5.9 3.1 %collective-permute-start.3 = (bf16[2,4,2,16,1536]{4,3,2,1,0:T(8,128)(2,1)S(1)}, bf16[2,4,2,16,1536]{4,3,2,1,0:T(8,128)(2,1)}, u32[]{:S(2)}, u32[]{:S(2)}) collective-permute-start(bf16[2,4,2,16,1536]{4,3,2,1,0:T(8,128)(2,1)S(1)} %get-tuple-element.67), channel_id=1, source_target_pairs={{0,3},{1,0},{2,1},{3,2},{4,7},{5,4},{6,5},{7,6},{8,11},{9,8},{10,9... | collective-permute-start | bytes 2359304 | tf_op jit(solution)/shard_map/ppermute | solution.py:22
  9.0 14.1 %collective-permute-done = bf16[2,4,2,16,1536]{4,3,1,0,2:T(8,128)(2,1)S(1)} collective-permute-done((bf16[2,4,2,16,1536]{4,3,1,0,2:T(8,128)(2,1)S(1)}, bf16[2,4,2,16,1536]{4,3,1,0,2:T(8,128)(2,1)S(1)}, u32[]{:S(2)}, u32[]{:S(2)}) %collective-permute-start) | collective-permute-done | bytes 786464 | tf_op jit(solution)/shard_map/ppermute | solution.py:22
  23.1 0.9 slice_bitcast_fusion.4
  24.1 3.0 %collective-permute-start.4 = (bf16[2,4,16,1536]{3,2,1,0:T(8,128)(2,1)}, bf16[2,4,16,1536]{3,2,1,0:T(8,128)(2,1)}, u32[]{:S(2)}, u32[]{:S(2)}) collective-permute-start(bf16[2,4,16,1536]{3,2,1,0:T(8,128)(2,1)} %get-tuple-element.69), channel_id=1, source_target_pairs={{0,3},{1,0},{2,1},{3,2},{4,7},{5,4},{6,5},{7,6},{8,11},{9,8},{10,9... | collective-permute-start | bytes 1179656 | tf_op jit(solution)/shard_map/ppermute | solution.py:22
  27.1 3.3 %collective-permute-start.7 = (bf16[2,4,2,16,1024]{4,3,1,0,2:T(8,128)(2,1)S(1)}, bf16[2,4,2,16,1024]{4,3,1,0,2:T(8,128)(2,1)S(1)}, u32[]{:S(2)}, u32[]{:S(2)}) collective-permute-start(bf16[2,4,2,16,1024]{4,3,1,0,2:T(8,128)(2,1)S(1)} %slice.45), channel_id=1, source_target_pairs={{0,4},{4,0},{1,5},{5,1},{2,6},{6,2},{3,7},{7,3},{8,12},{12,8},{9,1... | collective-permute-start | bytes 1572872 | tf_op jit(solution)/shard_map/ppermute | solution.py:22
  30.5 0.7 copy.7.starts_ref
  31.2 0.6 pad_add_fusion.place_ref
  31.8 0.9 copy.9.z_ref
  32.7 2.5 %collective-permute-done.4.xrc_ref = bf16[2,4,16,1536]{3,2,1,0:T(8,128)(2,1)} collective-permute-done((bf16[2,4,16,1536]{3,2,1,0:T(8,128)(2,1)}, bf16[2,4,16,1536]{3,2,1,0:T(8,128)(2,1)}, u32[]{:S(2)}, u32[]{:S(2)}) %collective-permute-start.4) | collective-permute-done | bytes 393248 | tf_op jit(solution)/shard_map/ppermute | solution.py:22
  35.2 3.4 %collective-permute-done.2.xlc_ref = bf16[2,4,16,1536]{3,2,1,0:T(8,128)(2,1)} collective-permute-done((bf16[2,4,16,1536]{3,2,1,0:T(8,128)(2,1)}, bf16[2,4,16,1536]{3,2,1,0:T(8,128)(2,1)}, u32[]{:S(2)}, u32[]{:S(2)}) %collective-permute-start.2) | collective-permute-done | bytes 393248 | tf_op jit(solution)/shard_map/ppermute | solution.py:22
  38.6 13.3 %attend.2 = (bf16[4,2,2,16,1536]{4,3,2,1,0:T(8,128)(2,1)}, bf16[2,4,2,2,16,1536]{5,4,3,2,1,0:T(8,128)(2,1)}, bf16[2,4,2,16,1536]{4,3,2,1,0:T(8,128)(2,1)}, bf16[...) custom-call(s32[2]{0:T(128)} %pad_add_fusion.place_ref, ...), custom_call_target="tpu_custom_call" | custom-call | flops 2400000000 | bytes 12582912 | tf_op jit(solution)/shard_map/attend/pallas_call | solution.py:255
  51.9 3.2 %collective-permute-start.17 = (bf16[2,4,16,1536]{3,2,1,0:T(8,128)(2,1)}, bf16[2,4,16,1536]{3,2,1,0:T(8,128)(2,1)S(1)}, u32[]{:S(2)}, u32[]{:S(2)}) collective-permute-start(bf16[2,4,16,1536]{3,2,1,0:T(8,128)(2,1)} %get-tuple-element.54), channel_id=1, source_target_pairs={{0,3},{1,0},{2,1},{3,2},{4,7},{5,4},{6,5},{7,6},{8,11},{9,8},{10,9... | collective-permute-start | bytes 1179656 | tf_op jit(solution)/shard_map/ppermute | solution.py:22
  55.2 0.1 collective-permute-start.12
  55.3 2.0 %collective-permute-start.10 = (bf16[2,4,16,1024]{3,2,1,0:T(8,128)(2,1)S(1)}, bf16[2,4,16,1024]{3,2,1,0:T(8,128)(2,1)}, u32[]{:S(2)}, u32[]{:S(2)}) collective-permute-start(bf16[2,4,16,1024]{3,2,1,0:T(8,128)(2,1)S(1)} %get-tuple-element.72), channel_id=1, source_target_pairs={{0,1},{1,2},{2,3},{3,0},{4,5},{5,6},{6,7},{7,4},{8,9},{9,10},{10,1... | collective-permute-start | bytes 786440 | tf_op jit(solution)/shard_map/ppermute | solution.py:22
  57.3 1.3 slice_bitcast_fusion.2
  58.7 6.7 %collective-permute-done.16.c0_ref = bf16[2,4,16,1536]{3,2,1,0:T(8,128)(2,1)S(1)} collective-permute-done((bf16[2,4,16,1536]{3,2,1,0:T(8,128)(2,1)}, bf16[2,4,16,1536]{3,2,1,0:T(8,128)(2,1)S(1)}, u32[]{:S(2)}, u32[]{:S(2)}) %collective-permute-start.16) | collective-permute-done | bytes 393248 | tf_op jit(solution)/shard_map/ppermute | solution.py:22
  65.4 2.0 %collective-permute-start.5 = (bf16[2,4,2,16,1536]{4,3,2,1,0:T(8,128)(2,1)}, bf16[2,4,2,16,1536]{4,3,2,1,0:T(8,128)(2,1)S(1)}, u32[]{:S(2)}, u32[]{:S(2)}) collective-permute-start(bf16[2,4,2,16,1536]{4,3,2,1,0:T(8,128)(2,1)} %get-tuple-element.35), channel_id=1, source_target_pairs={{0,1},{1,2},{2,3},{3,0},{4,5},{5,6},{6,7},{7,4},{8,9},{9,10},{10,1... | collective-permute-start | bytes 2359304 | tf_op jit(solution)/shard_map/ppermute | solution.py:22
  67.4 3.1 %collective-permute-done.12.xrc_ref = bf16[2,4,16,1024]{3,2,1,0:T(8,128)(2,1)S(1)} collective-permute-done((bf16[2,4,16,1024]{3,2,1,0:T(8,128)(2,1)S(1)}, bf16[2,4,16,1024]{3,2,1,0:T(8,128)(2,1)S(1)}, u32[]{:S(2)}, u32[]{:S(2)}) %collective-permute-start.12) | collective-permute-done | bytes 262176 | tf_op jit(solution)/shard_map/ppermute | solution.py:22
  70.6 3.7 %collective-permute-start.6 = (bf16[2,4,2,16,1536]{4,3,2,1,0:T(8,128)(2,1)}, bf16[2,4,2,16,1536]{4,3,2,1,0:T(8,128)(2,1)S(1)}, u32[]{:S(2)}, u32[]{:S(2)}) collective-permute-start(bf16[2,4,2,16,1536]{4,3,2,1,0:T(8,128)(2,1)} %get-tuple-element.36), channel_id=1, source_target_pairs={{0,3},{1,0},{2,1},{3,2},{4,7},{5,4},{6,5},{7,6},{8,11},{9,8},{10,9... | collective-permute-start | bytes 2359304 | tf_op jit(solution)/shard_map/ppermute | solution.py:22
  74.3 2.4 %corner_sum.2 = bf16[2,4,2,16,1536]{4,3,2,1,0:T(8,128)(2,1)} custom-call(bf16[2,4,2,16,1536]{4,3,2,1,0:T(8,128)(2,1)} %get-tuple-element.52.dz_ref, bf16[2,4,16,1536]{3,2,1,0:T(8,128)(2,1)} %copy-done.8, bf16[2,4,16,1536]{3,2,1,0:T(8,128)(2,1)} %copy-done.9), custom_call_target="tpu_custom_call" | custom-call | bytes 4194304 | tf_op jit(solution)/shard_map/corner_sum/pallas_call | solution.py:286
  76.7 5.6 %collective-permute-done.9.xl_ref = bf16[2,4,2,16,1024]{4,3,2,1,0:T(8,128)(2,1)S(1)} collective-permute-done((bf16[2,4,2,16,1024]{4,3,2,1,0:T(8,128)(2,1)S(1)}, bf16[2,4,2,16,1024]{4,3,2,1,0:T(8,128)(2,1)S(1)}, u32[]{:S(2)}, u32[]{:S(2)}) %collective-permute-start.9) | collective-permute-done | bytes 524320 | tf_op jit(solution)/shard_map/ppermute | solution.py:22
  82.3 0.9 copy.12.z_ref
  83.2 0.8 copy-done.5
  84.1 9.9 %attend.3 = (bf16[4,2,2,16,1024]{4,3,2,1,0:T(8,128)(2,1)}, bf16[2,4,2,2,16,1024]{5,4,3,2,1,0:T(8,128)(2,1)}, bf16[2,4,2,16,1024]{4,3,2,1,0:T(8,128)(2,1)}, bf16[...) custom-call(s32[2]{0:T(128)} %pad_add_fusion.place_ref, ...), custom_call_target="tpu_custom_call" | custom-call | flops 1600000000 | bytes 8388608 | tf_op jit(solution)/shard_map/attend/pallas_call | solution.py:255
  94.0 3.7 %collective-permute-start.15 = (bf16[4,2,2,16,1024]{4,3,2,1,0:T(8,128)(2,1)}, bf16[4,2,2,16,1024]{4,3,2,1,0:T(8,128)(2,1)S(1)}, u32[]{:S(2)}, u32[]{:S(2)}) collective-permute-start(bf16[4,2,2,16,1024]{4,3,2,1,0:T(8,128)(2,1)} %get-tuple-element.51), channel_id=1, source_target_pairs={{0,120},{8,0},{16,8},{24,16},{32,24},{40,32},{48,40},{56,48},{64,5... | collective-permute-start | bytes 1572872 | tf_op jit(solution)/shard_map/ppermute | solution.py:22
  97.7 0.9 copy-done.2
  98.6 0.2 copy-done.3
  98.8 3.3 %own_sum.2 = bf16[2,4,2,2,16,1536]{5,4,3,2,1,0:T(8,128)(2,1)} custom-call(bf16[2,4,2,2,16,1536]{5,4,3,2,1,0:T(8,128)(2,1)} %get-tuple-element.46.own_ref, bf16[2,4,2,16,1536]{4,3,2,1,0:T(8,128)(2,1)} %copy-done.2, bf16[2,4,2,16,1536]{4,3,2,1,0:T(8,128)(2,1)} %copy-done.3), custom_call_target="tpu_custom_call" | custom-call | bytes 5242880 | tf_op jit(solution)/shard_map/own_sum/pallas_call | solution.py:292
  102.1 3.2 %collective-permute-start.14 = (bf16[2,4,2,16,1024]{4,3,2,1,0:T(8,128)(2,1)S(1)}, bf16[2,4,2,16,1024]{4,3,2,1,0:T(8,128)(2,1)S(1)}, u32[]{:S(2)}, u32[]{:S(2)}) collective-permute-start(bf16[2,4,2,16,1024]{4,3,2,1,0:T(8,128)(2,1)S(1)} %copy-done.14), channel_id=1, source_target_pairs={{0,3},{1,0},{2,1},{3,2},{4,7},{5,4},{6,5},{7,6},{8,11},{9,8},{10,9... | collective-permute-start | bytes 1572872 | tf_op jit(solution)/shard_map/ppermute | solution.py:22
  105.4 4.4 %collective-permute-done.18 = bf16[2,4,2,16,1536]{4,3,2,1,0:T(8,128)(2,1)S(1)} collective-permute-done((bf16[2,4,2,16,1536]{4,3,2,1,0:T(8,128)(2,1)}, bf16[2,4,2,16,1536]{4,3,2,1,0:T(8,128)(2,1)S(1)}, u32[]{:S(2)}, u32[]{:S(2)}) %collective-permute-start.18) | collective-permute-done | bytes 786464 | tf_op jit(solution)/shard_map/ppermute | solution.py:31
  109.8 8.6 %collective-permute-done.13.r0_ref = bf16[2,4,2,16,1024]{4,3,2,1,0:T(8,128)(2,1)S(1)} collective-permute-done((bf16[2,4,2,16,1024]{4,3,2,1,0:T(8,128)(2,1)}, bf16[2,4,2,16,1024]{4,3,2,1,0:T(8,128)(2,1)S(1)}, u32[]{:S(2)}, u32[]{:S(2)}) %collective-permute-start.13) | collective-permute-done | bytes 524320 | tf_op jit(solution)/shard_map/ppermute | solution.py:22
  118.4 0.8 copy-done.6
  119.2 0.2 copy-done.7
  119.4 2.8 %own_sum.3 = bf16[2,4,2,2,16,1024]{5,4,3,2,1,0:T(8,128)(2,1)} custom-call(bf16[2,4,2,2,16,1024]{5,4,3,2,1,0:T(8,128)(2,1)} %get-tuple-element.56.own_ref, bf16[2,4,2,16,1024]{4,3,2,1,0:T(8,128)(2,1)} %copy-done.6, bf16[2,4,2,16,1024]{4,3,2,1,0:T(8,128)(2,1)} %copy-done.7), custom_call_target="tpu_custom_call" | custom-call | bytes 5242880 | tf_op jit(solution)/shard_map/own_sum/pallas_call | solution.py:292
  122.1 0.5 collective-permute-done.21.c0_ref
  122.6 0.7 copy-done.11
  123.3 0.1 copy-done.12
  123.4 2.1 %corner_sum.3 = bf16[2,4,2,16,1024]{4,3,2,1,0:T(8,128)(2,1)} custom-call(bf16[2,4,2,16,1024]{4,3,2,1,0:T(8,128)(2,1)} %get-tuple-element.60.dz_ref, bf16[2,4,16,1024]{3,2,1,0:T(8,128)(2,1)} %copy-done.11, bf16[2,4,16,1024]{3,2,1,0:T(8,128)(2,1)} %copy-done.12), custom_call_target="tpu_custom_call" | custom-call | bytes 4194304 | tf_op jit(solution)/shard_map/corner_sum/pallas_call | solution.py:286
  125.5 1.3 collective-permute-start.23
  126.8 0.1 maximum_bitcast_fusion.1
  126.9 21.8 %collective-permute-done.23 = bf16[2,4,2,16,1024]{4,3,2,1,0:T(8,128)(2,1)S(1)} collective-permute-done((bf16[2,4,2,16,1024]{4,3,2,1,0:T(8,128)(2,1)}, bf16[2,4,2,16,1024]{4,3,2,1,0:T(8,128)(2,1)S(1)}, u32[]{:S(2)}, u32[]{:S(2)}) %collective-permute-start.23) | collective-permute-done | bytes 524320 | tf_op jit(solution)/shard_map/ppermute | solution.py:31
  148.7 0.3 maximum_convert_fusion
  149.1 0.9 add_convert_fusion
  150.0 2.3 %maximum_bitcast_fusion = bf16[3,1,4,2,2,16,2560]{6,5,4,3,2,1,0:T(8,128)(2,1)} fusion(bf16[2,4,2,2,16,2560]{5,4,3,2,1,0:T(8,128)(2,1)S(1)} %add_convert_fusion, bf16[1,4,2,2,16,2560]{5,4,3,2,1,0:T(8,128)(2,1)S(1)} %maximum_bitcast_fusion.1), kind=kLoop, calls=%fused_computation.1 | loop fusion | flops 1966080 | bytes 7864320 | tf_op jit(solution)/shard_map/broadcast_in_dim | solution.py:303
  (55 shorter events, 0.4 us)
Async XLA Ops:
  0.0 5.6 %copy-start = (bf16[2,1,4,2,2,16,2560]{6,5,4,3,2,1,0:T(8,128)(2,1)S(1)}, bf16[2,1,4,2,2,16,2560]{6,5,4,3,2,1,0:T(8,128)(2,1)}, u32[]{:S(2)}) copy-start(bf16[2,1,4,2,2,16,2560]{6,5,4,3,2,1,0:T(8,128)(2,1)} %param.5) | copy-start | bytes 7864324
  1.6 21.5 %collective-permute-start = (bf16[2,4,2,16,1536]{4,3,1,0,2:T(8,128)(2,1)S(1)}, bf16[2,4,2,16,1536]{4,3,1,0,2:T(8,128)(2,1)S(1)}, u32[]{:S(2)}, u32[]{:S(2)}) collective-permute-start(bf16[2,4,2,16,1536]{4,3,1,0,2:T(8,128)(2,1)S(1)} %slice.40), channel_id=1, source_target_pairs={{0,4},{4,0},{1,5},{5,1},{2,6},{6,2},{3,7},{7,3},{8,12},{12,8},{9,1... | collective-permute-start | bytes 2359304 | tf_op jit(solution)/shard_map/ppermute | solution.py:22
  5.8 21.4 %copy-start.1 = (bf16[2,1,4,2,2,16,2560]{6,5,3,2,0,4,1:T(8,128)(2,1)}, bf16[2,1,4,2,2,16,2560]{6,5,3,2,0,4,1:T(8,128)(2,1)S(1)}, u32[]{:S(2)}) copy-start(bf16[2,1,4,2,2,16,2560]{6,5,3,2,0,4,1:T(8,128)(2,1)S(1)} %copy.17) | copy-start | bytes 7864324
  5.8 24.7 %copy-start.13 = (s32[4,2,2]{0,2,1:T(2,128)S(1)}, s32[4,2,2]{0,2,1:T(2,128)}, u32[]{:S(2)}) copy-start(s32[4,2,2]{0,2,1:T(2,128)} %param.7) | copy-start | bytes 196
  5.9 26.8 %collective-permute-start.3 = (bf16[2,4,2,16,1536]{4,3,2,1,0:T(8,128)(2,1)S(1)}, bf16[2,4,2,16,1536]{4,3,2,1,0:T(8,128)(2,1)}, u32[]{:S(2)}, u32[]{:S(2)}) collective-permute-start(bf16[2,4,2,16,1536]{4,3,2,1,0:T(8,128)(2,1)S(1)} %get-tuple-element.67), channel_id=1, source_target_pairs={{0,3},{1,0},{2,1},{3,2},{4,7},{5,4},{6,5},{7,6},{8,11},{9,8},{10,9... | collective-permute-start | bytes 2359304 | tf_op jit(solution)/shard_map/ppermute | solution.py:22
  9.0 23.7 %collective-permute-start.1 = (bf16[2,4,2,16,1536]{4,3,2,1,0:T(8,128)(2,1)S(1)}, bf16[2,4,2,16,1536]{4,3,2,1,0:T(8,128)(2,1)}, u32[]{:S(2)}, u32[]{:S(2)}) collective-permute-start(bf16[2,4,2,16,1536]{4,3,2,1,0:T(8,128)(2,1)S(1)} %get-tuple-element.68), channel_id=1, source_target_pairs={{0,1},{1,2},{2,3},{3,0},{4,5},{5,6},{6,7},{7,4},{8,9},{9,10},{10,1... | collective-permute-start | bytes 2359304 | tf_op jit(solution)/shard_map/ppermute | solution.py:22
  24.1 11.2 %collective-permute-start.4 = (bf16[2,4,16,1536]{3,2,1,0:T(8,128)(2,1)}, bf16[2,4,16,1536]{3,2,1,0:T(8,128)(2,1)}, u32[]{:S(2)}, u32[]{:S(2)}) collective-permute-start(bf16[2,4,16,1536]{3,2,1,0:T(8,128)(2,1)} %get-tuple-element.69), channel_id=1, source_target_pairs={{0,3},{1,0},{2,1},{3,2},{4,7},{5,4},{6,5},{7,6},{8,11},{9,8},{10,9... | collective-permute-start | bytes 1179656 | tf_op jit(solution)/shard_map/ppermute | solution.py:22
  27.1 11.5 %collective-permute-start.2 = (bf16[2,4,16,1536]{3,2,1,0:T(8,128)(2,1)}, bf16[2,4,16,1536]{3,2,1,0:T(8,128)(2,1)}, u32[]{:S(2)}, u32[]{:S(2)}) collective-permute-start(bf16[2,4,16,1536]{3,2,1,0:T(8,128)(2,1)} %get-tuple-element.70), channel_id=1, source_target_pairs={{0,1},{1,2},{2,3},{3,0},{4,5},{5,6},{6,7},{7,4},{8,9},{9,10},{10,1... | collective-permute-start | bytes 1179656 | tf_op jit(solution)/shard_map/ppermute | solution.py:22
  27.1 28.0 %collective-permute-start.7 = (bf16[2,4,2,16,1024]{4,3,1,0,2:T(8,128)(2,1)S(1)}, bf16[2,4,2,16,1024]{4,3,1,0,2:T(8,128)(2,1)S(1)}, u32[]{:S(2)}, u32[]{:S(2)}) collective-permute-start(bf16[2,4,2,16,1024]{4,3,1,0,2:T(8,128)(2,1)S(1)} %slice.45), channel_id=1, source_target_pairs={{0,4},{4,0},{1,5},{5,1},{2,6},{6,2},{3,7},{7,3},{8,12},{12,8},{9,1... | collective-permute-start | bytes 1572872 | tf_op jit(solution)/shard_map/ppermute | solution.py:22
  51.9 13.5 %collective-permute-start.16 = (bf16[2,4,16,1536]{3,2,1,0:T(8,128)(2,1)}, bf16[2,4,16,1536]{3,2,1,0:T(8,128)(2,1)S(1)}, u32[]{:S(2)}, u32[]{:S(2)}) collective-permute-start(bf16[2,4,16,1536]{3,2,1,0:T(8,128)(2,1)} %get-tuple-element.53), channel_id=1, source_target_pairs={{0,1},{1,2},{2,3},{3,0},{4,5},{5,6},{6,7},{7,4},{8,9},{9,10},{10,1... | collective-permute-start | bytes 1179656 | tf_op jit(solution)/shard_map/ppermute | solution.py:22
  51.9 13.5 %collective-permute-start.17 = (bf16[2,4,16,1536]{3,2,1,0:T(8,128)(2,1)}, bf16[2,4,16,1536]{3,2,1,0:T(8,128)(2,1)S(1)}, u32[]{:S(2)}, u32[]{:S(2)}) collective-permute-start(bf16[2,4,16,1536]{3,2,1,0:T(8,128)(2,1)} %get-tuple-element.54), channel_id=1, source_target_pairs={{0,3},{1,0},{2,1},{3,2},{4,7},{5,4},{6,5},{7,6},{8,11},{9,8},{10,9... | collective-permute-start | bytes 1179656 | tf_op jit(solution)/shard_map/ppermute | solution.py:22
  55.2 15.3 %collective-permute-start.12 = (bf16[2,4,16,1024]{3,2,1,0:T(8,128)(2,1)S(1)}, bf16[2,4,16,1024]{3,2,1,0:T(8,128)(2,1)S(1)}, u32[]{:S(2)}, u32[]{:S(2)}) collective-permute-start(bf16[2,4,16,1024]{3,2,1,0:T(8,128)(2,1)S(1)} %get-tuple-element.71), channel_id=1, source_target_pairs={{0,3},{1,0},{2,1},{3,2},{4,7},{5,4},{6,5},{7,6},{8,11},{9,8},{10,9... | collective-permute-start | bytes 786440 | tf_op jit(solution)/shard_map/ppermute | solution.py:22
  55.3 19.0 %collective-permute-start.10 = (bf16[2,4,16,1024]{3,2,1,0:T(8,128)(2,1)S(1)}, bf16[2,4,16,1024]{3,2,1,0:T(8,128)(2,1)}, u32[]{:S(2)}, u32[]{:S(2)}) collective-permute-start(bf16[2,4,16,1024]{3,2,1,0:T(8,128)(2,1)S(1)} %get-tuple-element.72), channel_id=1, source_target_pairs={{0,1},{1,2},{2,3},{3,0},{4,5},{5,6},{6,7},{7,4},{8,9},{9,10},{10,1... | collective-permute-start | bytes 786440 | tf_op jit(solution)/shard_map/ppermute | solution.py:22
  58.6 23.7 %collective-permute-start.9 = (bf16[2,4,2,16,1024]{4,3,2,1,0:T(8,128)(2,1)S(1)}, bf16[2,4,2,16,1024]{4,3,2,1,0:T(8,128)(2,1)S(1)}, u32[]{:S(2)}, u32[]{:S(2)}) collective-permute-start(bf16[2,4,2,16,1024]{4,3,2,1,0:T(8,128)(2,1)S(1)} %get-tuple-element.42), channel_id=1, source_target_pairs={{0,1},{1,2},{2,3},{3,0},{4,5},{5,6},{6,7},{7,4},{8,9},{9,10},{10,1... | collective-permute-start | bytes 1572872 | tf_op jit(solution)/shard_map/ppermute | solution.py:22
  65.4 8.9 %copy-start.8 = (bf16[2,4,16,1536]{3,2,1,0:T(8,128)(2,1)}, bf16[2,4,16,1536]{3,2,1,0:T(8,128)(2,1)S(1)}, u32[]{:S(2)}) copy-start(bf16[2,4,16,1536]{3,2,1,0:T(8,128)(2,1)S(1)} %collective-permute-done.16.c0_ref) | copy-start | bytes 1179652
  65.4 17.8 %collective-permute-start.11 = (bf16[2,4,2,16,1024]{4,3,2,1,0:T(8,128)(2,1)S(1)}, bf16[2,4,2,16,1024]{4,3,2,1,0:T(8,128)(2,1)S(1)}, u32[]{:S(2)}, u32[]{:S(2)}) collective-permute-start(bf16[2,4,2,16,1024]{4,3,2,1,0:T(8,128)(2,1)S(1)} %get-tuple-element.43), channel_id=1, source_target_pairs={{0,3},{1,0},{2,1},{3,2},{4,7},{5,4},{6,5},{7,6},{8,11},{9,8},{10,9... | collective-permute-start | bytes 1572872 | tf_op jit(solution)/shard_map/ppermute | solution.py:22
  65.4 8.9 %copy-start.9 = (bf16[2,4,16,1536]{3,2,1,0:T(8,128)(2,1)}, bf16[2,4,16,1536]{3,2,1,0:T(8,128)(2,1)S(1)}, u32[]{:S(2)}) copy-start(bf16[2,4,16,1536]{3,2,1,0:T(8,128)(2,1)S(1)} %collective-permute-done.17.c1_ref) | copy-start | bytes 1179652
  65.4 32.2 %collective-permute-start.5 = (bf16[2,4,2,16,1536]{4,3,2,1,0:T(8,128)(2,1)}, bf16[2,4,2,16,1536]{4,3,2,1,0:T(8,128)(2,1)S(1)}, u32[]{:S(2)}, u32[]{:S(2)}) collective-permute-start(bf16[2,4,2,16,1536]{4,3,2,1,0:T(8,128)(2,1)} %get-tuple-element.35), channel_id=1, source_target_pairs={{0,1},{1,2},{2,3},{3,0},{4,5},{5,6},{6,7},{7,4},{8,9},{9,10},{10,1... | collective-permute-start | bytes 2359304 | tf_op jit(solution)/shard_map/ppermute | solution.py:22
  70.6 6.1 %copy-start.10 = (bf16[2,4,16,1024]{3,2,1,0:T(8,128)(2,1)}, bf16[2,4,16,1024]{3,2,1,0:T(8,128)(2,1)S(1)}, u32[]{:S(2)}) copy-start(bf16[2,4,16,1024]{3,2,1,0:T(8,128)(2,1)S(1)} %collective-permute-done.12.xrc_ref) | copy-start | bytes 786436
  70.6 27.1 %collective-permute-start.6 = (bf16[2,4,2,16,1536]{4,3,2,1,0:T(8,128)(2,1)}, bf16[2,4,2,16,1536]{4,3,2,1,0:T(8,128)(2,1)S(1)}, u32[]{:S(2)}, u32[]{:S(2)}) collective-permute-start(bf16[2,4,2,16,1536]{4,3,2,1,0:T(8,128)(2,1)} %get-tuple-element.36), channel_id=1, source_target_pairs={{0,3},{1,0},{2,1},{3,2},{4,7},{5,4},{6,5},{7,6},{8,11},{9,8},{10,9... | collective-permute-start | bytes 2359304 | tf_op jit(solution)/shard_map/ppermute | solution.py:22
  74.3 23.4 %collective-permute-start.8 = (bf16[4,2,2,16,1536]{4,3,2,1,0:T(8,128)(2,1)}, bf16[4,2,2,16,1536]{4,3,2,1,0:T(8,128)(2,1)S(1)}, u32[]{:S(2)}, u32[]{:S(2)}) collective-permute-start(bf16[4,2,2,16,1536]{4,3,2,1,0:T(8,128)(2,1)} %get-tuple-element.39), channel_id=1, source_target_pairs={{0,120},{8,0},{16,8},{24,16},{32,24},{40,32},{48,40},{56,48},{64,5... | collective-permute-start | bytes 2359304 | tf_op jit(solution)/shard_map/ppermute | solution.py:22
  82.3 1.0 copy-start.4
  82.3 27.5 %collective-permute-start.18 = (bf16[2,4,2,16,1536]{4,3,2,1,0:T(8,128)(2,1)}, bf16[2,4,2,16,1536]{4,3,2,1,0:T(8,128)(2,1)S(1)}, u32[]{:S(2)}, u32[]{:S(2)}) collective-permute-start(bf16[2,4,2,16,1536]{4,3,2,1,0:T(8,128)(2,1)} %corner_sum.2), channel_id=1, source_target_pairs={{0,124},{4,120},{8,4},{12,0},{16,12},{20,8},{24,20},{28,16},{32,28... | collective-permute-start | bytes 2359304 | tf_op jit(solution)/shard_map/ppermute | solution.py:31
  83.2 0.8 copy-start.5
  94.0 8.2 %copy-start.14 = (bf16[2,4,2,16,1024]{4,3,2,1,0:T(8,128)(2,1)S(1)}, bf16[2,4,2,16,1024]{4,3,2,1,0:T(8,128)(2,1)}, u32[]{:S(2)}) copy-start(bf16[2,4,2,16,1024]{4,3,2,1,0:T(8,128)(2,1)} %get-tuple-element.50) | copy-start | bytes 1572868
  94.0 15.9 %copy-start.15 = (bf16[2,4,16,1024]{3,2,1,0:T(8,128)(2,1)S(1)}, bf16[2,4,16,1024]{3,2,1,0:T(8,128)(2,1)}, u32[]{:S(2)}) copy-start(bf16[2,4,16,1024]{3,2,1,0:T(8,128)(2,1)} %get-tuple-element.64) | copy-start | bytes 786436
  94.0 11.4 %collective-permute-start.15 = (bf16[4,2,2,16,1024]{4,3,2,1,0:T(8,128)(2,1)}, bf16[4,2,2,16,1024]{4,3,2,1,0:T(8,128)(2,1)S(1)}, u32[]{:S(2)}, u32[]{:S(2)}) collective-permute-start(bf16[4,2,2,16,1024]{4,3,2,1,0:T(8,128)(2,1)} %get-tuple-element.51), channel_id=1, source_target_pairs={{0,120},{8,0},{16,8},{24,16},{32,24},{40,32},{48,40},{56,48},{64,5... | collective-permute-start | bytes 1572872 | tf_op jit(solution)/shard_map/ppermute | solution.py:22
  97.6 0.9 copy-start.2
  97.7 1.1 copy-start.3
  102.1 16.3 %collective-permute-start.13 = (bf16[2,4,2,16,1024]{4,3,2,1,0:T(8,128)(2,1)}, bf16[2,4,2,16,1024]{4,3,2,1,0:T(8,128)(2,1)S(1)}, u32[]{:S(2)}, u32[]{:S(2)}) collective-permute-start(bf16[2,4,2,16,1024]{4,3,2,1,0:T(8,128)(2,1)} %get-tuple-element.49), channel_id=1, source_target_pairs={{0,1},{1,2},{2,3},{3,0},{4,5},{5,6},{6,7},{7,4},{8,9},{9,10},{10,1... | collective-permute-start | bytes 1572872 | tf_op jit(solution)/shard_map/ppermute | solution.py:22
  102.1 16.3 %collective-permute-start.14 = (bf16[2,4,2,16,1024]{4,3,2,1,0:T(8,128)(2,1)S(1)}, bf16[2,4,2,16,1024]{4,3,2,1,0:T(8,128)(2,1)S(1)}, u32[]{:S(2)}, u32[]{:S(2)}) collective-permute-start(bf16[2,4,2,16,1024]{4,3,2,1,0:T(8,128)(2,1)S(1)} %copy-done.14), channel_id=1, source_target_pairs={{0,3},{1,0},{2,1},{3,2},{4,7},{5,4},{6,5},{7,6},{8,11},{9,8},{10,9... | collective-permute-start | bytes 1572872 | tf_op jit(solution)/shard_map/ppermute | solution.py:22
  105.4 43.7 %collective-permute-start.19 = (bf16[2,4,2,2,16,1536]{5,4,3,2,1,0:T(8,128)(2,1)}, bf16[2,4,2,2,16,1536]{5,4,3,2,1,0:T(8,128)(2,1)S(1)}, u32[]{:S(2)}, u32[]{:S(2)}) collective-permute-start(bf16[2,4,2,2,16,1536]{5,4,3,2,1,0:T(8,128)(2,1)} %own_sum.2), channel_id=1, source_target_pairs={{0,120},{8,0},{16,8},{24,16},{32,24},{40,32},{48,40},{56,48},{64,5... | collective-permute-start | bytes 4718600 | tf_op jit(solution)/shard_map/ppermute | solution.py:22
  105.4 17.2 %collective-permute-start.21 = (bf16[2,4,16,1024]{3,2,1,0:T(8,128)(2,1)}, bf16[2,4,16,1024]{3,2,1,0:T(8,128)(2,1)S(1)}, u32[]{:S(2)}, u32[]{:S(2)}) collective-permute-start(bf16[2,4,16,1024]{3,2,1,0:T(8,128)(2,1)} %get-tuple-element.63), channel_id=1, source_target_pairs={{0,1},{1,2},{2,3},{3,0},{4,5},{5,6},{6,7},{7,4},{8,9},{9,10},{10,1... | collective-permute-start | bytes 786440 | tf_op jit(solution)/shard_map/ppermute | solution.py:22
  109.8 12.8 %collective-permute-start.22 = (bf16[2,4,16,1024]{3,2,1,0:T(8,128)(2,1)S(1)}, bf16[2,4,16,1024]{3,2,1,0:T(8,128)(2,1)S(1)}, u32[]{:S(2)}, u32[]{:S(2)}) collective-permute-start(bf16[2,4,16,1024]{3,2,1,0:T(8,128)(2,1)S(1)} %copy-done.15), channel_id=1, source_target_pairs={{0,3},{1,0},{2,1},{3,2},{4,7},{5,4},{6,5},{7,6},{8,11},{9,8},{10,9... | collective-permute-start | bytes 786440 | tf_op jit(solution)/shard_map/ppermute | solution.py:22
  118.4 0.8 copy-start.6
  118.4 1.0 copy-start.7
  122.1 26.9 %collective-permute-start.20 = (bf16[2,4,2,2,16,1024]{5,4,3,2,1,0:T(8,128)(2,1)}, bf16[2,4,2,2,16,1024]{5,4,3,2,1,0:T(8,128)(2,1)S(1)}, u32[]{:S(2)}, u32[]{:S(2)}) collective-permute-start(bf16[2,4,2,2,16,1024]{5,4,3,2,1,0:T(8,128)(2,1)} %own_sum.3), channel_id=1, source_target_pairs={{0,120},{8,0},{16,8},{24,16},{32,24},{40,32},{48,40},{56,48},{64,5... | collective-permute-start | bytes 3145736 | tf_op jit(solution)/shard_map/ppermute | solution.py:22
  122.6 0.7 copy-start.11
  122.6 0.8 copy-start.12
  125.5 23.2 %collective-permute-start.23 = (bf16[2,4,2,16,1024]{4,3,2,1,0:T(8,128)(2,1)}, bf16[2,4,2,16,1024]{4,3,2,1,0:T(8,128)(2,1)S(1)}, u32[]{:S(2)}, u32[]{:S(2)}) collective-permute-start(bf16[2,4,2,16,1024]{4,3,2,1,0:T(8,128)(2,1)} %corner_sum.3), channel_id=1, source_target_pairs={{0,124},{4,120},{8,4},{12,0},{16,12},{20,8},{24,20},{28,16},{32,28... | collective-permute-start | bytes 1572872 | tf_op jit(solution)/shard_map/ppermute | solution.py:31

commit v3 on v1

--- a/solution.py
+++ b/solution.py
@@ -161,8 +161,9 @@
             )
             dz_ref[s, :, :, :, cols] = d_own[s][n_kv:].reshape(times, 2, tok, HEAD_DIM)
             d0, d1 = d_x[s]
-            left = (jnp.where(first, 0.0, d0) + jnp.where(last, d1, 0.0)).astype(BF)
-            right = (jnp.where(last, 0.0, d1) + jnp.where(first, d0, 0.0)).astype(BF)
+            both, none = (d0 + d1).astype(BF), jnp.zeros_like(d0, BF)
+            left = jnp.where(first, none, jnp.where(last, both, d0.astype(BF)))
+            right = jnp.where(last, none, jnp.where(first, both, d1.astype(BF)))
             for value, ref, corner in ((left, dxl_ref, dxlc_ref), (right, dxr_ref, dxrc_ref)):
                 ref[s, :, :, :, cols] = value[:n_row].reshape(times, 2, tok, HEAD_DIM)
                 corner[s, :, :, cols] = value[n_row:].reshape(times, tok, HEAD_DIM)

time: 153 us -> 153 us (level)
  no operation moved by 1% of the time
where the time goes in v3:
time: 153 us; the launch traced here: 152 us
  waiting for transfers between devices  70.5 us (46%)
  Pallas kernels  34.2 us (22%)
  starting transfers between devices  32.6 us (21%)
  local copies, waits for them, and re-layouts  10.7 us (7%)
  other arithmetic  4.19 us (3%)
    ppermute x22, waiting for transfers between devices, shift(): lax.ppermute(block, axis, [(i, (i + step) % count) for i in range(count)])  44.4 us
    ppermute x22, starting transfers between devices, shift(): lax.ppermute(block, axis, [(i, (i + step) % count) for i in range(count)])  31.5 us
    ppermute x2, waiting for transfers between devices, shift_across(): return lax.ppermute(block, ('section', 'ha'), route)  26.1 us
    pallas_call x2, Pallas kernels, local(): call(functools.partial(attend, base), [SMEM, SMEM] + [VMEM] * 8, [sd((tim...  23.3 us
    pallas_call x2, Pallas kernels, local(): call(own_sum, [VMEM] * 3, sd((2, times, 2, 2, tok, width), BF), 'own_sum'...  6.09 us
    pallas_call x2, Pallas kernels, local(): call(corner_sum, [VMEM] * 3, sd((2, *body), BF), 'corner_sum', moved=4 *...  4.84 us
    unnamed x34, local copies, waits for them, and re-layouts  4.74 us
  transfers between devices with their start and end apart: 24, of which 10 were waited for; matrix products, arithmetic and copies ran while one was open for 4% of the time, Pallas kernels for 22%

profile of v3, /device:TPU:6, one launch (start us, length us, event | category | flops | bytes accessed | tf_op | source)
XLA Modules:
  0.0 152.4 jit_solution(15342024859894664837)
XLA Ops:
  0.0 1.6 %copy_bitcast_fusion.1 = bf16[2,4,2,16,2560]{4,3,1,0,2:T(8,128)(2,1)S(1)} fusion(bf16[2,1,4,2,2,16,2560]{6,5,4,3,2,1,0:T(8,128)(2,1)} %param.5, s32[]{:T(128)S(6)} %select_n.8), kind=kLoop, calls=%fused_computation.5 | loop fusion | bytes 2621444 | tf_op jit(solution)/shard_map/jit(dynamic_index_in_dim)/squeeze | solution.py:220
  1.6 4.0 %collective-permute-start = (bf16[2,4,2,16,1536]{4,3,1,0,2:T(8,128)(2,1)S(1)}, bf16[2,4,2,16,1536]{4,3,1,0,2:T(8,128)(2,1)S(1)}, u32[]{:S(2)}, u32[]{:S(2)}) collective-permute-start(bf16[2,4,2,16,1536]{4,3,1,0,2:T(8,128)(2,1)S(1)} %slice.40), channel_id=1, source_target_pairs={{0,4},{4,0},{1,5},{5,1},{2,6},{6,2},{3,7},{7,3},{8,12},{12,8},{9,1... | collective-permute-start | bytes 2359304 | tf_op jit(solution)/shard_map/ppermute | solution.py:22
  5.6 0.2 copy.17
  5.8 0.1 slice_bitcast_fusion
  5.9 3.1 %collective-permute-start.3 = (bf16[2,4,2,16,1536]{4,3,2,1,0:T(8,128)(2,1)S(1)}, bf16[2,4,2,16,1536]{4,3,2,1,0:T(8,128)(2,1)}, u32[]{:S(2)}, u32[]{:S(2)}) collective-permute-start(bf16[2,4,2,16,1536]{4,3,2,1,0:T(8,128)(2,1)S(1)} %get-tuple-element.67), channel_id=1, source_target_pairs={{0,3},{1,0},{2,1},{3,2},{4,7},{5,4},{6,5},{7,6},{8,11},{9,8},{10,9... | collective-permute-start | bytes 2359304 | tf_op jit(solution)/shard_map/ppermute | solution.py:22
  9.0 14.1 %collective-permute-done = bf16[2,4,2,16,1536]{4,3,1,0,2:T(8,128)(2,1)S(1)} collective-permute-done((bf16[2,4,2,16,1536]{4,3,1,0,2:T(8,128)(2,1)S(1)}, bf16[2,4,2,16,1536]{4,3,1,0,2:T(8,128)(2,1)S(1)}, u32[]{:S(2)}, u32[]{:S(2)}) %collective-permute-start) | collective-permute-done | bytes 786464 | tf_op jit(solution)/shard_map/ppermute | solution.py:22
  23.1 0.9 slice_bitcast_fusion.4
  24.1 3.0 %collective-permute-start.4 = (bf16[2,4,16,1536]{3,2,1,0:T(8,128)(2,1)}, bf16[2,4,16,1536]{3,2,1,0:T(8,128)(2,1)}, u32[]{:S(2)}, u32[]{:S(2)}) collective-permute-start(bf16[2,4,16,1536]{3,2,1,0:T(8,128)(2,1)} %get-tuple-element.69), channel_id=1, source_target_pairs={{0,3},{1,0},{2,1},{3,2},{4,7},{5,4},{6,5},{7,6},{8,11},{9,8},{10,9... | collective-permute-start | bytes 1179656 | tf_op jit(solution)/shard_map/ppermute | solution.py:22
  27.1 3.3 %collective-permute-start.7 = (bf16[2,4,2,16,1024]{4,3,1,0,2:T(8,128)(2,1)S(1)}, bf16[2,4,2,16,1024]{4,3,1,0,2:T(8,128)(2,1)S(1)}, u32[]{:S(2)}, u32[]{:S(2)}) collective-permute-start(bf16[2,4,2,16,1024]{4,3,1,0,2:T(8,128)(2,1)S(1)} %slice.45), channel_id=1, source_target_pairs={{0,4},{4,0},{1,5},{5,1},{2,6},{6,2},{3,7},{7,3},{8,12},{12,8},{9,1... | collective-permute-start | bytes 1572872 | tf_op jit(solution)/shard_map/ppermute | solution.py:22
  30.5 0.7 copy.7.starts_ref
  31.1 0.7 pad_add_fusion.place_ref
  31.8 1.0 copy.9.z_ref
  32.8 2.4 %collective-permute-done.4.xrc_ref = bf16[2,4,16,1536]{3,2,1,0:T(8,128)(2,1)} collective-permute-done((bf16[2,4,16,1536]{3,2,1,0:T(8,128)(2,1)}, bf16[2,4,16,1536]{3,2,1,0:T(8,128)(2,1)}, u32[]{:S(2)}, u32[]{:S(2)}) %collective-permute-start.4) | collective-permute-done | bytes 393248 | tf_op jit(solution)/shard_map/ppermute | solution.py:22
  35.2 3.4 %collective-permute-done.2.xlc_ref = bf16[2,4,16,1536]{3,2,1,0:T(8,128)(2,1)} collective-permute-done((bf16[2,4,16,1536]{3,2,1,0:T(8,128)(2,1)}, bf16[2,4,16,1536]{3,2,1,0:T(8,128)(2,1)}, u32[]{:S(2)}, u32[]{:S(2)}) %collective-permute-start.2) | collective-permute-done | bytes 393248 | tf_op jit(solution)/shard_map/ppermute | solution.py:22
  38.6 13.3 %attend.2 = (bf16[4,2,2,16,1536]{4,3,2,1,0:T(8,128)(2,1)}, bf16[2,4,2,2,16,1536]{5,4,3,2,1,0:T(8,128)(2,1)}, f32[2,4,2,16,1536]{4,3,2,1,0:T(8,128)}, bf16[2,4,2,...) custom-call(s32[2]{0:T(128)} %pad_add_fusion.place_ref, ...), custom_call_target="tpu_custom_call" | custom-call | flops 2400000000 | bytes 12582912 | tf_op jit(solution)/shard_map/attend/pallas_call | solution.py:256
  52.0 3.2 %collective-permute-start.17 = (bf16[2,4,16,1536]{3,2,1,0:T(8,128)(2,1)}, bf16[2,4,16,1536]{3,2,1,0:T(8,128)(2,1)S(1)}, u32[]{:S(2)}, u32[]{:S(2)}) collective-permute-start(bf16[2,4,16,1536]{3,2,1,0:T(8,128)(2,1)} %get-tuple-element.54), channel_id=1, source_target_pairs={{0,3},{1,0},{2,1},{3,2},{4,7},{5,4},{6,5},{7,6},{8,11},{9,8},{10,9... | collective-permute-start | bytes 1179656 | tf_op jit(solution)/shard_map/ppermute | solution.py:22
  55.4 2.0 %collective-permute-start.10 = (bf16[2,4,16,1024]{3,2,1,0:T(8,128)(2,1)S(1)}, bf16[2,4,16,1024]{3,2,1,0:T(8,128)(2,1)}, u32[]{:S(2)}, u32[]{:S(2)}) collective-permute-start(bf16[2,4,16,1024]{3,2,1,0:T(8,128)(2,1)S(1)} %get-tuple-element.72), channel_id=1, source_target_pairs={{0,1},{1,2},{2,3},{3,0},{4,5},{5,6},{6,7},{7,4},{8,9},{9,10},{10,1... | collective-permute-start | bytes 786440 | tf_op jit(solution)/shard_map/ppermute | solution.py:22
  57.4 1.3 slice_bitcast_fusion.2
  58.7 6.7 %collective-permute-done.16.c0_ref = bf16[2,4,16,1536]{3,2,1,0:T(8,128)(2,1)S(1)} collective-permute-done((bf16[2,4,16,1536]{3,2,1,0:T(8,128)(2,1)}, bf16[2,4,16,1536]{3,2,1,0:T(8,128)(2,1)S(1)}, u32[]{:S(2)}, u32[]{:S(2)}) %collective-permute-start.16) | collective-permute-done | bytes 393248 | tf_op jit(solution)/shard_map/ppermute | solution.py:22
  65.5 2.0 %collective-permute-start.5 = (bf16[2,4,2,16,1536]{4,3,2,1,0:T(8,128)(2,1)}, bf16[2,4,2,16,1536]{4,3,2,1,0:T(8,128)(2,1)S(1)}, u32[]{:S(2)}, u32[]{:S(2)}) collective-permute-start(bf16[2,4,2,16,1536]{4,3,2,1,0:T(8,128)(2,1)} %get-tuple-element.35), channel_id=1, source_target_pairs={{0,1},{1,2},{2,3},{3,0},{4,5},{5,6},{6,7},{7,4},{8,9},{9,10},{10,1... | collective-permute-start | bytes 2359304 | tf_op jit(solution)/shard_map/ppermute | solution.py:22
  67.5 3.1 %collective-permute-done.12.xrc_ref = bf16[2,4,16,1024]{3,2,1,0:T(8,128)(2,1)S(1)} collective-permute-done((bf16[2,4,16,1024]{3,2,1,0:T(8,128)(2,1)S(1)}, bf16[2,4,16,1024]{3,2,1,0:T(8,128)(2,1)S(1)}, u32[]{:S(2)}, u32[]{:S(2)}) %collective-permute-start.12) | collective-permute-done | bytes 262176 | tf_op jit(solution)/shard_map/ppermute | solution.py:22
  70.6 3.7 %collective-permute-start.6 = (bf16[2,4,2,16,1536]{4,3,2,1,0:T(8,128)(2,1)}, bf16[2,4,2,16,1536]{4,3,2,1,0:T(8,128)(2,1)S(1)}, u32[]{:S(2)}, u32[]{:S(2)}) collective-permute-start(bf16[2,4,2,16,1536]{4,3,2,1,0:T(8,128)(2,1)} %get-tuple-element.36), channel_id=1, source_target_pairs={{0,3},{1,0},{2,1},{3,2},{4,7},{5,4},{6,5},{7,6},{8,11},{9,8},{10,9... | collective-permute-start | bytes 2359304 | tf_op jit(solution)/shard_map/ppermute | solution.py:22
  74.3 2.6 %corner_sum.2 = bf16[2,4,2,16,1536]{4,3,2,1,0:T(8,128)(2,1)} custom-call(f32[2,4,2,16,1536]{4,3,2,1,0:T(8,128)} %get-tuple-element.52.dz_ref, bf16[2,4,16,1536]{3,2,1,0:T(8,128)(2,1)} %copy-done.8, bf16[2,4,16,1536]{3,2,1,0:T(8,128)(2,1)} %copy-done.9), custom_call_target="tpu_custom_call" | custom-call | bytes 4194304 | tf_op jit(solution)/shard_map/corner_sum/pallas_call | solution.py:287
  77.0 5.4 %collective-permute-done.9.xl_ref = bf16[2,4,2,16,1024]{4,3,2,1,0:T(8,128)(2,1)S(1)} collective-permute-done((bf16[2,4,2,16,1024]{4,3,2,1,0:T(8,128)(2,1)S(1)}, bf16[2,4,2,16,1024]{4,3,2,1,0:T(8,128)(2,1)S(1)}, u32[]{:S(2)}, u32[]{:S(2)}) %collective-permute-start.9) | collective-permute-done | bytes 524320 | tf_op jit(solution)/shard_map/ppermute | solution.py:22
  82.3 0.9 copy.12.z_ref
  83.3 0.1 copy-done.4
  83.3 0.8 copy-done.5
  84.1 10.0 %attend.3 = (bf16[4,2,2,16,1024]{4,3,2,1,0:T(8,128)(2,1)}, bf16[2,4,2,2,16,1024]{5,4,3,2,1,0:T(8,128)(2,1)}, f32[2,4,2,16,1024]{4,3,2,1,0:T(8,128)}, bf16[2,4,2,...) custom-call(s32[2]{0:T(128)} %pad_add_fusion.place_ref, ...), custom_call_target="tpu_custom_call" | custom-call | flops 1600000000 | bytes 8388608 | tf_op jit(solution)/shard_map/attend/pallas_call | solution.py:256
  94.2 3.7 %collective-permute-start.15 = (bf16[4,2,2,16,1024]{4,3,2,1,0:T(8,128)(2,1)}, bf16[4,2,2,16,1024]{4,3,2,1,0:T(8,128)(2,1)S(1)}, u32[]{:S(2)}, u32[]{:S(2)}) collective-permute-start(bf16[4,2,2,16,1024]{4,3,2,1,0:T(8,128)(2,1)} %get-tuple-element.51), channel_id=1, source_target_pairs={{0,120},{8,0},{16,8},{24,16},{32,24},{40,32},{48,40},{56,48},{64,5... | collective-permute-start | bytes 1572872 | tf_op jit(solution)/shard_map/ppermute | solution.py:22
  97.8 0.9 copy-done.2
  98.7 0.3 copy-done.3
  99.0 3.3 %own_sum.2 = bf16[2,4,2,2,16,1536]{5,4,3,2,1,0:T(8,128)(2,1)} custom-call(bf16[2,4,2,2,16,1536]{5,4,3,2,1,0:T(8,128)(2,1)} %get-tuple-element.46.own_ref, bf16[2,4,2,16,1536]{4,3,2,1,0:T(8,128)(2,1)} %copy-done.2, bf16[2,4,2,16,1536]{4,3,2,1,0:T(8,128)(2,1)} %copy-done.3), custom_call_target="tpu_custom_call" | custom-call | bytes 5242880 | tf_op jit(solution)/shard_map/own_sum/pallas_call | solution.py:293
  102.4 3.2 %collective-permute-start.14 = (bf16[2,4,2,16,1024]{4,3,2,1,0:T(8,128)(2,1)S(1)}, bf16[2,4,2,16,1024]{4,3,2,1,0:T(8,128)(2,1)S(1)}, u32[]{:S(2)}, u32[]{:S(2)}) collective-permute-start(bf16[2,4,2,16,1024]{4,3,2,1,0:T(8,128)(2,1)S(1)} %copy-done.14), channel_id=1, source_target_pairs={{0,3},{1,0},{2,1},{3,2},{4,7},{5,4},{6,5},{7,6},{8,11},{9,8},{10,9... | collective-permute-start | bytes 1572872 | tf_op jit(solution)/shard_map/ppermute | solution.py:22
  105.6 4.2 %collective-permute-done.18 = bf16[2,4,2,16,1536]{4,3,2,1,0:T(8,128)(2,1)S(1)} collective-permute-done((bf16[2,4,2,16,1536]{4,3,2,1,0:T(8,128)(2,1)}, bf16[2,4,2,16,1536]{4,3,2,1,0:T(8,128)(2,1)S(1)}, u32[]{:S(2)}, u32[]{:S(2)}) %collective-permute-start.18) | collective-permute-done | bytes 786464 | tf_op jit(solution)/shard_map/ppermute | solution.py:31
  109.9 8.8 %collective-permute-done.13.r0_ref = bf16[2,4,2,16,1024]{4,3,2,1,0:T(8,128)(2,1)S(1)} collective-permute-done((bf16[2,4,2,16,1024]{4,3,2,1,0:T(8,128)(2,1)}, bf16[2,4,2,16,1024]{4,3,2,1,0:T(8,128)(2,1)S(1)}, u32[]{:S(2)}, u32[]{:S(2)}) %collective-permute-start.13) | collective-permute-done | bytes 524320 | tf_op jit(solution)/shard_map/ppermute | solution.py:22
  118.6 0.8 copy-done.6
  119.4 0.2 copy-done.7
  119.6 2.8 %own_sum.3 = bf16[2,4,2,2,16,1024]{5,4,3,2,1,0:T(8,128)(2,1)} custom-call(bf16[2,4,2,2,16,1024]{5,4,3,2,1,0:T(8,128)(2,1)} %get-tuple-element.56.own_ref, bf16[2,4,2,16,1024]{4,3,2,1,0:T(8,128)(2,1)} %copy-done.6, bf16[2,4,2,16,1024]{4,3,2,1,0:T(8,128)(2,1)} %copy-done.7), custom_call_target="tpu_custom_call" | custom-call | bytes 5242880 | tf_op jit(solution)/shard_map/own_sum/pallas_call | solution.py:293
  122.4 0.4 collective-permute-done.21.c0_ref
  122.8 0.7 copy-done.11
  123.5 0.1 copy-done.12
  123.6 2.2 %corner_sum.3 = bf16[2,4,2,16,1024]{4,3,2,1,0:T(8,128)(2,1)} custom-call(f32[2,4,2,16,1024]{4,3,2,1,0:T(8,128)} %get-tuple-element.60.dz_ref, bf16[2,4,16,1024]{3,2,1,0:T(8,128)(2,1)} %copy-done.11, bf16[2,4,16,1024]{3,2,1,0:T(8,128)(2,1)} %copy-done.12), custom_call_target="tpu_custom_call" | custom-call | bytes 4194304 | tf_op jit(solution)/shard_map/corner_sum/pallas_call | solution.py:287
  125.8 1.2 collective-permute-start.23
  127.0 0.1 maximum_bitcast_fusion.1
  127.1 21.8 %collective-permute-done.23 = bf16[2,4,2,16,1024]{4,3,2,1,0:T(8,128)(2,1)S(1)} collective-permute-done((bf16[2,4,2,16,1024]{4,3,2,1,0:T(8,128)(2,1)}, bf16[2,4,2,16,1024]{4,3,2,1,0:T(8,128)(2,1)S(1)}, u32[]{:S(2)}, u32[]{:S(2)}) %collective-permute-start.23) | collective-permute-done | bytes 524320 | tf_op jit(solution)/shard_map/ppermute | solution.py:31
  148.9 0.3 maximum_convert_fusion
  149.3 0.9 add_convert_fusion
  150.2 2.3 %maximum_bitcast_fusion = bf16[3,1,4,2,2,16,2560]{6,5,4,3,2,1,0:T(8,128)(2,1)} fusion(bf16[2,4,2,2,16,2560]{5,4,3,2,1,0:T(8,128)(2,1)S(1)} %add_convert_fusion, bf16[1,4,2,2,16,2560]{5,4,3,2,1,0:T(8,128)(2,1)S(1)} %maximum_bitcast_fusion.1), kind=kLoop, calls=%fused_computation.1 | loop fusion | flops 1966080 | bytes 7864320 | tf_op jit(solution)/shard_map/broadcast_in_dim | solution.py:304
  (55 shorter events, 0.5 us)
Async XLA Ops:
  0.0 5.6 %copy-start = (bf16[2,1,4,2,2,16,2560]{6,5,4,3,2,1,0:T(8,128)(2,1)S(1)}, bf16[2,1,4,2,2,16,2560]{6,5,4,3,2,1,0:T(8,128)(2,1)}, u32[]{:S(2)}) copy-start(bf16[2,1,4,2,2,16,2560]{6,5,4,3,2,1,0:T(8,128)(2,1)} %param.5) | copy-start | bytes 7864324
  1.6 21.5 %collective-permute-start = (bf16[2,4,2,16,1536]{4,3,1,0,2:T(8,128)(2,1)S(1)}, bf16[2,4,2,16,1536]{4,3,1,0,2:T(8,128)(2,1)S(1)}, u32[]{:S(2)}, u32[]{:S(2)}) collective-permute-start(bf16[2,4,2,16,1536]{4,3,1,0,2:T(8,128)(2,1)S(1)} %slice.40), channel_id=1, source_target_pairs={{0,4},{4,0},{1,5},{5,1},{2,6},{6,2},{3,7},{7,3},{8,12},{12,8},{9,1... | collective-permute-start | bytes 2359304 | tf_op jit(solution)/shard_map/ppermute | solution.py:22
  5.8 21.4 %copy-start.1 = (bf16[2,1,4,2,2,16,2560]{6,5,3,2,0,4,1:T(8,128)(2,1)}, bf16[2,1,4,2,2,16,2560]{6,5,3,2,0,4,1:T(8,128)(2,1)S(1)}, u32[]{:S(2)}) copy-start(bf16[2,1,4,2,2,16,2560]{6,5,3,2,0,4,1:T(8,128)(2,1)S(1)} %copy.17) | copy-start | bytes 7864324
  5.8 24.7 %copy-start.13 = (s32[4,2,2]{0,2,1:T(2,128)S(1)}, s32[4,2,2]{0,2,1:T(2,128)}, u32[]{:S(2)}) copy-start(s32[4,2,2]{0,2,1:T(2,128)} %param.7) | copy-start | bytes 196
  5.9 26.9 %collective-permute-start.3 = (bf16[2,4,2,16,1536]{4,3,2,1,0:T(8,128)(2,1)S(1)}, bf16[2,4,2,16,1536]{4,3,2,1,0:T(8,128)(2,1)}, u32[]{:S(2)}, u32[]{:S(2)}) collective-permute-start(bf16[2,4,2,16,1536]{4,3,2,1,0:T(8,128)(2,1)S(1)} %get-tuple-element.67), channel_id=1, source_target_pairs={{0,3},{1,0},{2,1},{3,2},{4,7},{5,4},{6,5},{7,6},{8,11},{9,8},{10,9... | collective-permute-start | bytes 2359304 | tf_op jit(solution)/shard_map/ppermute | solution.py:22
  9.0 23.8 %collective-permute-start.1 = (bf16[2,4,2,16,1536]{4,3,2,1,0:T(8,128)(2,1)S(1)}, bf16[2,4,2,16,1536]{4,3,2,1,0:T(8,128)(2,1)}, u32[]{:S(2)}, u32[]{:S(2)}) collective-permute-start(bf16[2,4,2,16,1536]{4,3,2,1,0:T(8,128)(2,1)S(1)} %get-tuple-element.68), channel_id=1, source_target_pairs={{0,1},{1,2},{2,3},{3,0},{4,5},{5,6},{6,7},{7,4},{8,9},{9,10},{10,1... | collective-permute-start | bytes 2359304 | tf_op jit(solution)/shard_map/ppermute | solution.py:22
  24.1 11.2 %collective-permute-start.4 = (bf16[2,4,16,1536]{3,2,1,0:T(8,128)(2,1)}, bf16[2,4,16,1536]{3,2,1,0:T(8,128)(2,1)}, u32[]{:S(2)}, u32[]{:S(2)}) collective-permute-start(bf16[2,4,16,1536]{3,2,1,0:T(8,128)(2,1)} %get-tuple-element.69), channel_id=1, source_target_pairs={{0,3},{1,0},{2,1},{3,2},{4,7},{5,4},{6,5},{7,6},{8,11},{9,8},{10,9... | collective-permute-start | bytes 1179656 | tf_op jit(solution)/shard_map/ppermute | solution.py:22
  27.1 11.5 %collective-permute-start.2 = (bf16[2,4,16,1536]{3,2,1,0:T(8,128)(2,1)}, bf16[2,4,16,1536]{3,2,1,0:T(8,128)(2,1)}, u32[]{:S(2)}, u32[]{:S(2)}) collective-permute-start(bf16[2,4,16,1536]{3,2,1,0:T(8,128)(2,1)} %get-tuple-element.70), channel_id=1, source_target_pairs={{0,1},{1,2},{2,3},{3,0},{4,5},{5,6},{6,7},{7,4},{8,9},{9,10},{10,1... | collective-permute-start | bytes 1179656 | tf_op jit(solution)/shard_map/ppermute | solution.py:22
  27.1 28.1 %collective-permute-start.7 = (bf16[2,4,2,16,1024]{4,3,1,0,2:T(8,128)(2,1)S(1)}, bf16[2,4,2,16,1024]{4,3,1,0,2:T(8,128)(2,1)S(1)}, u32[]{:S(2)}, u32[]{:S(2)}) collective-permute-start(bf16[2,4,2,16,1024]{4,3,1,0,2:T(8,128)(2,1)S(1)} %slice.45), channel_id=1, source_target_pairs={{0,4},{4,0},{1,5},{5,1},{2,6},{6,2},{3,7},{7,3},{8,12},{12,8},{9,1... | collective-permute-start | bytes 1572872 | tf_op jit(solution)/shard_map/ppermute | solution.py:22
  51.9 13.5 %collective-permute-start.16 = (bf16[2,4,16,1536]{3,2,1,0:T(8,128)(2,1)}, bf16[2,4,16,1536]{3,2,1,0:T(8,128)(2,1)S(1)}, u32[]{:S(2)}, u32[]{:S(2)}) collective-permute-start(bf16[2,4,16,1536]{3,2,1,0:T(8,128)(2,1)} %get-tuple-element.53), channel_id=1, source_target_pairs={{0,1},{1,2},{2,3},{3,0},{4,5},{5,6},{6,7},{7,4},{8,9},{9,10},{10,1... | collective-permute-start | bytes 1179656 | tf_op jit(solution)/shard_map/ppermute | solution.py:22
  52.0 13.5 %collective-permute-start.17 = (bf16[2,4,16,1536]{3,2,1,0:T(8,128)(2,1)}, bf16[2,4,16,1536]{3,2,1,0:T(8,128)(2,1)S(1)}, u32[]{:S(2)}, u32[]{:S(2)}) collective-permute-start(bf16[2,4,16,1536]{3,2,1,0:T(8,128)(2,1)} %get-tuple-element.54), channel_id=1, source_target_pairs={{0,3},{1,0},{2,1},{3,2},{4,7},{5,4},{6,5},{7,6},{8,11},{9,8},{10,9... | collective-permute-start | bytes 1179656 | tf_op jit(solution)/shard_map/ppermute | solution.py:22
  55.3 15.3 %collective-permute-start.12 = (bf16[2,4,16,1024]{3,2,1,0:T(8,128)(2,1)S(1)}, bf16[2,4,16,1024]{3,2,1,0:T(8,128)(2,1)S(1)}, u32[]{:S(2)}, u32[]{:S(2)}) collective-permute-start(bf16[2,4,16,1024]{3,2,1,0:T(8,128)(2,1)S(1)} %get-tuple-element.71), channel_id=1, source_target_pairs={{0,3},{1,0},{2,1},{3,2},{4,7},{5,4},{6,5},{7,6},{8,11},{9,8},{10,9... | collective-permute-start | bytes 786440 | tf_op jit(solution)/shard_map/ppermute | solution.py:22
  55.4 19.0 %collective-permute-start.10 = (bf16[2,4,16,1024]{3,2,1,0:T(8,128)(2,1)S(1)}, bf16[2,4,16,1024]{3,2,1,0:T(8,128)(2,1)}, u32[]{:S(2)}, u32[]{:S(2)}) collective-permute-start(bf16[2,4,16,1024]{3,2,1,0:T(8,128)(2,1)S(1)} %get-tuple-element.72), channel_id=1, source_target_pairs={{0,1},{1,2},{2,3},{3,0},{4,5},{5,6},{6,7},{7,4},{8,9},{9,10},{10,1... | collective-permute-start | bytes 786440 | tf_op jit(solution)/shard_map/ppermute | solution.py:22
  58.7 23.7 %collective-permute-start.9 = (bf16[2,4,2,16,1024]{4,3,2,1,0:T(8,128)(2,1)S(1)}, bf16[2,4,2,16,1024]{4,3,2,1,0:T(8,128)(2,1)S(1)}, u32[]{:S(2)}, u32[]{:S(2)}) collective-permute-start(bf16[2,4,2,16,1024]{4,3,2,1,0:T(8,128)(2,1)S(1)} %get-tuple-element.42), channel_id=1, source_target_pairs={{0,1},{1,2},{2,3},{3,0},{4,5},{5,6},{6,7},{7,4},{8,9},{9,10},{10,1... | collective-permute-start | bytes 1572872 | tf_op jit(solution)/shard_map/ppermute | solution.py:22
  65.5 8.9 %copy-start.8 = (bf16[2,4,16,1536]{3,2,1,0:T(8,128)(2,1)}, bf16[2,4,16,1536]{3,2,1,0:T(8,128)(2,1)S(1)}, u32[]{:S(2)}) copy-start(bf16[2,4,16,1536]{3,2,1,0:T(8,128)(2,1)S(1)} %collective-permute-done.16.c0_ref) | copy-start | bytes 1179652
  65.5 17.8 %collective-permute-start.11 = (bf16[2,4,2,16,1024]{4,3,2,1,0:T(8,128)(2,1)S(1)}, bf16[2,4,2,16,1024]{4,3,2,1,0:T(8,128)(2,1)S(1)}, u32[]{:S(2)}, u32[]{:S(2)}) collective-permute-start(bf16[2,4,2,16,1024]{4,3,2,1,0:T(8,128)(2,1)S(1)} %get-tuple-element.43), channel_id=1, source_target_pairs={{0,3},{1,0},{2,1},{3,2},{4,7},{5,4},{6,5},{7,6},{8,11},{9,8},{10,9... | collective-permute-start | bytes 1572872 | tf_op jit(solution)/shard_map/ppermute | solution.py:22
  65.5 8.9 %copy-start.9 = (bf16[2,4,16,1536]{3,2,1,0:T(8,128)(2,1)}, bf16[2,4,16,1536]{3,2,1,0:T(8,128)(2,1)S(1)}, u32[]{:S(2)}) copy-start(bf16[2,4,16,1536]{3,2,1,0:T(8,128)(2,1)S(1)} %collective-permute-done.17.c1_ref) | copy-start | bytes 1179652
  65.5 32.3 %collective-permute-start.5 = (bf16[2,4,2,16,1536]{4,3,2,1,0:T(8,128)(2,1)}, bf16[2,4,2,16,1536]{4,3,2,1,0:T(8,128)(2,1)S(1)}, u32[]{:S(2)}, u32[]{:S(2)}) collective-permute-start(bf16[2,4,2,16,1536]{4,3,2,1,0:T(8,128)(2,1)} %get-tuple-element.35), channel_id=1, source_target_pairs={{0,1},{1,2},{2,3},{3,0},{4,5},{5,6},{6,7},{7,4},{8,9},{9,10},{10,1... | collective-permute-start | bytes 2359304 | tf_op jit(solution)/shard_map/ppermute | solution.py:22
  70.6 6.3 %copy-start.10 = (bf16[2,4,16,1024]{3,2,1,0:T(8,128)(2,1)}, bf16[2,4,16,1024]{3,2,1,0:T(8,128)(2,1)S(1)}, u32[]{:S(2)}) copy-start(bf16[2,4,16,1024]{3,2,1,0:T(8,128)(2,1)S(1)} %collective-permute-done.12.xrc_ref) | copy-start | bytes 786436
  70.6 27.2 %collective-permute-start.6 = (bf16[2,4,2,16,1536]{4,3,2,1,0:T(8,128)(2,1)}, bf16[2,4,2,16,1536]{4,3,2,1,0:T(8,128)(2,1)S(1)}, u32[]{:S(2)}, u32[]{:S(2)}) collective-permute-start(bf16[2,4,2,16,1536]{4,3,2,1,0:T(8,128)(2,1)} %get-tuple-element.36), channel_id=1, source_target_pairs={{0,3},{1,0},{2,1},{3,2},{4,7},{5,4},{6,5},{7,6},{8,11},{9,8},{10,9... | collective-permute-start | bytes 2359304 | tf_op jit(solution)/shard_map/ppermute | solution.py:22
  74.3 23.5 %collective-permute-start.8 = (bf16[4,2,2,16,1536]{4,3,2,1,0:T(8,128)(2,1)}, bf16[4,2,2,16,1536]{4,3,2,1,0:T(8,128)(2,1)S(1)}, u32[]{:S(2)}, u32[]{:S(2)}) collective-permute-start(bf16[4,2,2,16,1536]{4,3,2,1,0:T(8,128)(2,1)} %get-tuple-element.39), channel_id=1, source_target_pairs={{0,120},{8,0},{16,8},{24,16},{32,24},{40,32},{48,40},{56,48},{64,5... | collective-permute-start | bytes 2359304 | tf_op jit(solution)/shard_map/ppermute | solution.py:22
  82.3 1.0 copy-start.4
  82.3 27.5 %collective-permute-start.18 = (bf16[2,4,2,16,1536]{4,3,2,1,0:T(8,128)(2,1)}, bf16[2,4,2,16,1536]{4,3,2,1,0:T(8,128)(2,1)S(1)}, u32[]{:S(2)}, u32[]{:S(2)}) collective-permute-start(bf16[2,4,2,16,1536]{4,3,2,1,0:T(8,128)(2,1)} %corner_sum.2), channel_id=1, source_target_pairs={{0,124},{4,120},{8,4},{12,0},{16,12},{20,8},{24,20},{28,16},{32,28... | collective-permute-start | bytes 2359304 | tf_op jit(solution)/shard_map/ppermute | solution.py:31
  83.3 0.8 copy-start.5
  94.1 8.2 %copy-start.14 = (bf16[2,4,2,16,1024]{4,3,2,1,0:T(8,128)(2,1)S(1)}, bf16[2,4,2,16,1024]{4,3,2,1,0:T(8,128)(2,1)}, u32[]{:S(2)}) copy-start(bf16[2,4,2,16,1024]{4,3,2,1,0:T(8,128)(2,1)} %get-tuple-element.50) | copy-start | bytes 1572868
  94.2 15.7 %copy-start.15 = (bf16[2,4,16,1024]{3,2,1,0:T(8,128)(2,1)S(1)}, bf16[2,4,16,1024]{3,2,1,0:T(8,128)(2,1)}, u32[]{:S(2)}) copy-start(bf16[2,4,16,1024]{3,2,1,0:T(8,128)(2,1)} %get-tuple-element.64) | copy-start | bytes 786436
  94.2 11.4 %collective-permute-start.15 = (bf16[4,2,2,16,1024]{4,3,2,1,0:T(8,128)(2,1)}, bf16[4,2,2,16,1024]{4,3,2,1,0:T(8,128)(2,1)S(1)}, u32[]{:S(2)}, u32[]{:S(2)}) collective-permute-start(bf16[4,2,2,16,1024]{4,3,2,1,0:T(8,128)(2,1)} %get-tuple-element.51), channel_id=1, source_target_pairs={{0,120},{8,0},{16,8},{24,16},{32,24},{40,32},{48,40},{56,48},{64,5... | collective-permute-start | bytes 1572872 | tf_op jit(solution)/shard_map/ppermute | solution.py:22
  97.8 0.9 copy-start.2
  97.8 1.2 copy-start.3
  102.3 16.3 %collective-permute-start.13 = (bf16[2,4,2,16,1024]{4,3,2,1,0:T(8,128)(2,1)}, bf16[2,4,2,16,1024]{4,3,2,1,0:T(8,128)(2,1)S(1)}, u32[]{:S(2)}, u32[]{:S(2)}) collective-permute-start(bf16[2,4,2,16,1024]{4,3,2,1,0:T(8,128)(2,1)} %get-tuple-element.49), channel_id=1, source_target_pairs={{0,1},{1,2},{2,3},{3,0},{4,5},{5,6},{6,7},{7,4},{8,9},{9,10},{10,1... | collective-permute-start | bytes 1572872 | tf_op jit(solution)/shard_map/ppermute | solution.py:22
  102.4 16.3 %collective-permute-start.14 = (bf16[2,4,2,16,1024]{4,3,2,1,0:T(8,128)(2,1)S(1)}, bf16[2,4,2,16,1024]{4,3,2,1,0:T(8,128)(2,1)S(1)}, u32[]{:S(2)}, u32[]{:S(2)}) collective-permute-start(bf16[2,4,2,16,1024]{4,3,2,1,0:T(8,128)(2,1)S(1)} %copy-done.14), channel_id=1, source_target_pairs={{0,3},{1,0},{2,1},{3,2},{4,7},{5,4},{6,5},{7,6},{8,11},{9,8},{10,9... | collective-permute-start | bytes 1572872 | tf_op jit(solution)/shard_map/ppermute | solution.py:22
  105.6 43.7 %collective-permute-start.19 = (bf16[2,4,2,2,16,1536]{5,4,3,2,1,0:T(8,128)(2,1)}, bf16[2,4,2,2,16,1536]{5,4,3,2,1,0:T(8,128)(2,1)S(1)}, u32[]{:S(2)}, u32[]{:S(2)}) collective-permute-start(bf16[2,4,2,2,16,1536]{5,4,3,2,1,0:T(8,128)(2,1)} %own_sum.2), channel_id=1, source_target_pairs={{0,120},{8,0},{16,8},{24,16},{32,24},{40,32},{48,40},{56,48},{64,5... | collective-permute-start | bytes 4718600 | tf_op jit(solution)/shard_map/ppermute | solution.py:22
  105.6 17.2 %collective-permute-start.21 = (bf16[2,4,16,1024]{3,2,1,0:T(8,128)(2,1)}, bf16[2,4,16,1024]{3,2,1,0:T(8,128)(2,1)S(1)}, u32[]{:S(2)}, u32[]{:S(2)}) collective-permute-start(bf16[2,4,16,1024]{3,2,1,0:T(8,128)(2,1)} %get-tuple-element.63), channel_id=1, source_target_pairs={{0,1},{1,2},{2,3},{3,0},{4,5},{5,6},{6,7},{7,4},{8,9},{9,10},{10,1... | collective-permute-start | bytes 786440 | tf_op jit(solution)/shard_map/ppermute | solution.py:22
  109.8 12.9 %collective-permute-start.22 = (bf16[2,4,16,1024]{3,2,1,0:T(8,128)(2,1)S(1)}, bf16[2,4,16,1024]{3,2,1,0:T(8,128)(2,1)S(1)}, u32[]{:S(2)}, u32[]{:S(2)}) collective-permute-start(bf16[2,4,16,1024]{3,2,1,0:T(8,128)(2,1)S(1)} %copy-done.15), channel_id=1, source_target_pairs={{0,3},{1,0},{2,1},{3,2},{4,7},{5,4},{6,5},{7,6},{8,11},{9,8},{10,9... | collective-permute-start | bytes 786440 | tf_op jit(solution)/shard_map/ppermute | solution.py:22
  118.6 0.8 copy-start.6
  118.6 1.0 copy-start.7
  122.4 26.9 %collective-permute-start.20 = (bf16[2,4,2,2,16,1024]{5,4,3,2,1,0:T(8,128)(2,1)}, bf16[2,4,2,2,16,1024]{5,4,3,2,1,0:T(8,128)(2,1)S(1)}, u32[]{:S(2)}, u32[]{:S(2)}) collective-permute-start(bf16[2,4,2,2,16,1024]{5,4,3,2,1,0:T(8,128)(2,1)} %own_sum.3), channel_id=1, source_target_pairs={{0,120},{8,0},{16,8},{24,16},{32,24},{40,32},{48,40},{56,48},{64,5... | collective-permute-start | bytes 3145736 | tf_op jit(solution)/shard_map/ppermute | solution.py:22
  122.8 0.7 copy-start.11
  122.8 0.8 copy-start.12
  125.8 23.1 %collective-permute-start.23 = (bf16[2,4,2,16,1024]{4,3,2,1,0:T(8,128)(2,1)}, bf16[2,4,2,16,1024]{4,3,2,1,0:T(8,128)(2,1)S(1)}, u32[]{:S(2)}, u32[]{:S(2)}) collective-permute-start(bf16[2,4,2,16,1024]{4,3,2,1,0:T(8,128)(2,1)} %corner_sum.3), channel_id=1, source_target_pairs={{0,124},{4,120},{8,4},{12,0},{16,12},{20,8},{24,20},{28,16},{32,28... | collective-permute-start | bytes 1572872 | tf_op jit(solution)/shard_map/ppermute | solution.py:31
